TPU v7x, 32 devices: a whole 2x2x4 slice. The times are simulated.
32 devices in a mesh: sys: 2 (over y), row: 4 (over z), col: 4 (over x, core).
Axes of the slice: x: 2, y: 2, z: 4, core: 2. Of those that a mesh axis runs over, the one named last changes fastest.
Arguments:
- blocks: bfloat16 [8, 4, 16, 128, 128], P(('sys', 'row'), 'col'), parts along dimension 0, may hold values from -0.8984375 to 0.8984375
- pairs: int32 [8, 4, 16, 16, 2], P(('sys', 'row'), 'col'), parts along dimension 0, may hold values from 0 to 63, as said below
- term_count: int32 [8, 4, 16], P(('sys', 'row'), 'col'), parts along dimension 0, may hold values from 1 to 16
Outputs:
- purified: bfloat16 [8, 4, 16, 128, 128], P(('sys', 'row'), 'col'), parts along dimension 0
There are 2 independent parts, one for each index of `sys`. A program takes and returns all parts, laid end to end along the dimension named above; each array names one. Nothing has to cross between parts.
Inputs may be any that keep to these rules, and one draw needn't show every extreme that they name: pairs[..., 0] is below 64 and pairs[..., 1] is below 64. For each grid position (r, c) and each r', the entries pairs[r, c, :, :, 1] that lie in [r' * 16, (r' + 1) * 16) take at most 8 distinct values, all terms counted, active or not; some grid position reaches 8 for some r'.
All inputs are finite; a program needn't handle non-finite values.
Results may differ from a plain program's by a relative error of at most 0.0048.
Values may be sent and summed in bfloat16 or wider, within the bound.
No kernel may reach another device: no remote copies, remote signals or barrier semaphores. Data moves between devices by JAX's collectives and lax.ppermute only.
A program may use at most 128 MiB of HBM per device.

v0:
```python
import jax
import jax.numpy as jnp
from jax import lax
from jax.sharding import PartitionSpec as P

CAP = 8


def stacked_product(left_panel, right_panel, left_index, right_index, active):
    slot_count, term_total = active.shape
    extent = left_panel.shape[-1]
    left_stack = jnp.take(left_panel, left_index.reshape(-1), axis=0).reshape(
        slot_count, term_total, extent, extent
    )
    left_stack = jnp.where(active[:, :, None, None], left_stack, jnp.zeros((), left_stack.dtype))
    right_stack = jnp.take(right_panel, right_index.reshape(-1), axis=0).reshape(
        slot_count, term_total, extent, extent
    )
    return jnp.einsum("stij,stjk->sik", left_stack, right_stack, preferred_element_type=jnp.float32)


def per_device(blocks, pairs, term_count):
    extent = blocks.shape[-1]
    slot_count = blocks.shape[2]
    term_total = pairs.shape[3]
    row_gathered = lax.all_gather(blocks, "col", axis=1, tiled=True).reshape(-1, extent, extent)
    pairing = pairs.reshape(slot_count, term_total, 2)
    left_index = pairing[:, :, 0]
    right_index = pairing[:, :, 1]
    grid_rows = lax.axis_size("row")
    flat_index = right_index.reshape(-1)
    source = flat_index // slot_count
    slot = flat_index % slot_count
    hits = (source[:, None, None] == jnp.arange(grid_rows, dtype=jnp.int32)[None, :, None]) & (
        slot[:, None, None] == jnp.arange(slot_count, dtype=jnp.int32)[None, None, :]
    )
    used = jnp.any(hits, axis=0)
    ranking = jnp.cumsum(used.astype(jnp.int32), axis=1) - 1
    select = used[:, :, None] & (
        ranking[:, :, None] == jnp.arange(CAP, dtype=jnp.int32)[None, None, :]
    )
    request = jnp.sum(
        select.astype(jnp.int32) * jnp.arange(slot_count, dtype=jnp.int32)[None, :, None], axis=1
    )
    asked = lax.all_to_all(request, "row", split_axis=0, concat_axis=0, tiled=True)
    local_blocks = blocks.reshape(slot_count, extent, extent)
    reply = jnp.take(local_blocks, asked.reshape(-1), axis=0).reshape(
        grid_rows, CAP, extent, extent
    )
    column_gathered = lax.all_to_all(reply, "row", split_axis=0, concat_axis=0, tiled=True).reshape(
        -1, extent, extent
    )
    column_index = (source * CAP + jnp.take(ranking.reshape(-1), flat_index)).reshape(
        slot_count, term_total
    )
    active = (
        jnp.arange(term_total, dtype=jnp.int32)[None, :] < term_count.reshape(slot_count)[:, None]
    )
    square = stacked_product(row_gathered, column_gathered, left_index, column_index, active)
    square_stored = square.astype(jnp.bfloat16).reshape(blocks.shape)
    square_gathered = lax.all_gather(square_stored, "col", axis=1, tiled=True).reshape(
        -1, extent, extent
    )
    cubed = stacked_product(square_gathered, column_gathered, left_index, column_index, active)
    purified = (3.0 * square - 2.0 * cubed).astype(jnp.bfloat16)
    return purified.reshape(blocks.shape)


def solution(mesh):
    placed = (
        P(("sys", "row"), "col", None, None, None),
        P(("sys", "row"), "col", None, None, None),
        P(("sys", "row"), "col", None),
    )
    return jax.shard_map(
        per_device,
        mesh=mesh,
        in_specs=placed,
        out_specs=P(("sys", "row"), "col", None, None, None),
        check_vma=False,
    )
```

profile of v0, /device:TPU:0, one launch (start us, length us, event | category | flops | bytes accessed | tf_op | source)
XLA Modules:
  0.0 150.8 jit_solution(16960238675948629166)
XLA Ops:
  6.5 0.8 slice_reduce_fusion
  7.4 0.1 reshape_squeeze.10
  7.5 0.2 and_reduce_fusion
  7.7 0.2 reduce_window_sum.11
  7.9 0.7 select_reduce_fusion
  8.6 6.3 %all-to-all-start = ((s32[4,1,8]{2,1,0:T(1,128)}), s32[4,1,8]{2,1,0:T(1,128)S(1)}, u32[]{:S(2)}, u32[]{:S(2)}) async-start(s32[4,1,8]{2,1,0:T(1,128)} %bitcast.7), calls=%async_computation | async-start | bytes 4096 | tf_op jit(solution)/shard_map/all_to_all | solution.py:45
  14.9 0.0 all-gather.4.cloned.1.call-start
  14.9 0.7 all-gather.4.cloned.1.call-update
  15.6 4.7 %all-to-all-done = s32[4,1,8]{2,1,0:T(1,128)S(1)} async-done(((s32[4,1,8]{2,1,0:T(1,128)}), s32[4,1,8]{2,1,0:T(1,128)S(1)}, u32[]{:S(2)}, u32[]{:S(2)}) %all-to-all-start) | async-done | bytes 160 | tf_op jit(solution)/shard_map/all_to_all | solution.py:45
  20.4 0.5 broadcast.210
  20.9 0.7 reduce.13
  21.6 0.1 reshape.254
  21.7 1.8 %gather_fusion = bf16[32,128,128]{2,1,0:T(8,128)(2,1)S(1)} fusion(bf16[16,128,128]{2,1,0:T(8,128)(2,1)} %bitcast.43, s32[1024]{0:T(1024)S(1)} %pad_clamp_fusion.1), kind=kCustom, calls=%fused_computation.3 | custom fusion | bytes 2097280 | tf_op jit(solution)/shard_map/jit(_take)/gather | solution.py:47
  23.5 1.2 broadcast_select_fusion.3
  24.6 3.5 %all-to-all-start.1 = ((bf16[4,8,128,128]{3,2,1,0:T(8,128)(2,1)}), bf16[4,8,128,128]{3,2,1,0:T(8,128)(2,1)S(1)}, u32[]{:S(2)}, u32[]{:S(2)}) async-start(bf16[4,8,128,128]{3,2,1,0:T(8,128)(2,1)} %broadcast_select_fusion.3), calls=%async_computation.1 | async-start | bytes 2097152 | tf_op jit(solution)/shard_map/all_to_all | solution.py:50
  28.2 0.0 all-gather.6.cloned.1.call-start
  28.2 0.1 sub.17
  28.3 0.1 reshape_squeeze.9
  28.4 0.1 reshape_squeeze.11
  28.5 1.9 %gather_fusion.1 = s32[256]{0:T(256)S(1)} fusion(s32[64]{0:T(128)S(1)} %sub.17, s32[1024]{0:T(1024)S(1)} %pad_clamp_fusion.2), kind=kCustom, calls=%fused_computation.4 | custom fusion | bytes 3072 | tf_op jit(solution)/shard_map/jit(_take)/gather | solution.py:53
  30.4 0.7 iota_compare_fusion.2
  31.2 21.5 %all-to-all-done.1 = bf16[4,8,128,128]{3,2,1,0:T(8,128)(2,1)S(1)} async-done(((bf16[4,8,128,128]{3,2,1,0:T(8,128)(2,1)}), bf16[4,8,128,128]{3,2,1,0:T(8,128)(2,1)S(1)}, u32[]{:S(2)}, u32[]{:S(2)}) %all-to-all-start.1) | async-done | bytes 1048608 | tf_op jit(solution)/shard_map/all_to_all | solution.py:50
  52.7 8.6 %gather_fusion.3 = bf16[256,128,128]{2,1,0:T(8,128)(2,1)} fusion(bf16[32,128,128]{2,1,0:T(8,128)(2,1)S(1)} %bitcast.36, s32[1024]{0:T(1024)S(1)} %pad_clamp_fusion), kind=kCustom, calls=%fused_computation.1.clone | custom fusion | bytes 16778240 | tf_op jit(solution)/shard_map/jit(_take)/gather | solution.py:16
  61.3 7.4 %broadcast_select_fusion = bf16[256,128,128]{2,1,0:T(8,128)(2,1)} fusion(bf16[256,128,128]{2,1,0:T(8,128)(2,1)} %gather_fusion.3, pred[256]{0:T(512)(128)(4,1)S(1)} %get-tuple-element.9), kind=kLoop, calls=%fused_computation.9 | loop fusion | flops 4194304 | bytes 16777472 | tf_op jit(solution)/shard_map/jit(_take)/select_n | solution.py:16
  68.7 10.2 %gather_fusion.2 = bf16[256,128,128]{2,1,0:T(8,128)(2,1)} fusion(bf16[64,128,128]{2,1,0:T(8,128)(2,1)} %bitcast.37, s32[1024]{0:T(1024)S(1)} %pad_clamp_fusion.3), kind=kCustom, calls=%fused_computation.clone | custom fusion | bytes 16778240 | tf_op jit(solution)/shard_map/jit(_take)/gather | solution.py:12
  78.9 7.4 %broadcast_select_fusion.2 = bf16[256,128,128]{2,1,0:T(8,128)(2,1)} fusion(bf16[256,128,128]{2,1,0:T(8,128)(2,1)} %gather_fusion.2, pred[256]{0:T(512)(128)(4,1)S(1)} %compare_and_fusion.1), kind=kLoop, calls=%fused_computation.11 | loop fusion | flops 4194304 | bytes 16777472 | tf_op jit(solution)/shard_map/jit(_take)/select_n | solution.py:12
  86.3 9.0 %fusion.31 = (bf16[16,128,128]{2,1,0:T(8,128)(2,1)}, f32[16,128,128]{2,1,0:T(8,128)S(1)}) fusion(bf16[16,16,128,128]{3,2,1,0:T(8,128)(2,1)} %bitcast.38, bf16[16,16,128,128]{3,2,1,0:T(8,128)(2,1)} %bitcast.41, pred[16,16]{1,0:T(8,128)(4,1)S(1)} %iota_compare_fusion.2), kind=kOutput, calls=%fused_computation.58 | convolution fusion | flops 1078198272 | bytes 18350336 | tf_op jit(solution)/shard_map/stij,stjk->sik/dot_general | solution.py:19
  95.3 0.0 all-gather.6.cloned.1.call-update
  95.3 21.9 %all-gather.6.cloned.1.call-done = bf16[64,128,128]{2,1,0:T(8,128)(2,1)} async-done(((bf16[16,128,128]{2,1,0:T(8,128)(2,1)}), bf16[64,128,128]{2,1,0:T(8,128)(2,1)}) %all-gather.6.cloned.1.call-update) | async-done | bytes 2097168 | tf_op jit(solution)/shard_map/all_gather | solution.py:61
  117.2 10.4 %gather_fusion.4 = bf16[256,128,128]{2,1,0:T(8,128)(2,1)} fusion(bf16[64,128,128]{2,1,0:T(8,128)(2,1)} %all-gather.6.cloned.1.call-done, s32[1024]{0:T(1024)S(1)} %pad_clamp_fusion.3), kind=kCustom, calls=%fused_computation.2.clone | custom fusion | bytes 16778240 | tf_op jit(solution)/shard_map/jit(_take)/gather | solution.py:12
  127.6 7.4 %broadcast_select_fusion.1 = bf16[256,128,128]{2,1,0:T(8,128)(2,1)} fusion(bf16[256,128,128]{2,1,0:T(8,128)(2,1)} %gather_fusion.4, pred[256]{0:T(512)(128)(4,1)S(1)} %compare_and_fusion.1), kind=kLoop, calls=%fused_computation.10 | loop fusion | flops 4194304 | bytes 16777472 | tf_op jit(solution)/shard_map/jit(_take)/select_n | solution.py:12
  135.0 9.0 %fusion.23 = bf16[1,1,16,128,128]{4,3,2,1,0:T(8,128)(2,1)} fusion(bf16[16,16,128,128]{3,2,1,0:T(8,128)(2,1)} %bitcast.39, bf16[16,16,128,128]{3,2,1,0:T(8,128)(2,1)} %bitcast.40, pred[16,16]{1,0:T(8,128)(4,1)S(1)} %iota_compare_fusion.2, f32[16,128,128]{2,1,0:T(8,128)S(1)} %get-tuple-element.15), kind=kOutput, calls=%fused_computation.21 | convolution fusion | flops 1078984704 | bytes 18350336 | tf_op jit(solution)/shard_map/stij,stjk->sik/dot_general | solution.py:19
  (16 shorter events, 0.1 us)
Async XLA Ops:
  8.6 11.8 %all-to-all-start = ((s32[4,1,8]{2,1,0:T(1,128)}), s32[4,1,8]{2,1,0:T(1,128)S(1)}, u32[]{:S(2)}, u32[]{:S(2)}) async-start(s32[4,1,8]{2,1,0:T(1,128)} %bitcast.7), calls=%async_computation | async-start | bytes 4096 | tf_op jit(solution)/shard_map/all_to_all | solution.py:45
  14.9 53.8 %all-gather.4.cloned.1.call-start = ((), (), s32[]{:S(2)}) async-start(), calls=%async_computation.2 | async-start | bytes 2621440 | tf_op jit(solution)/shard_map/all_gather | solution.py:26
  24.6 28.1 %all-to-all-start.1 = ((bf16[4,8,128,128]{3,2,1,0:T(8,128)(2,1)}), bf16[4,8,128,128]{3,2,1,0:T(8,128)(2,1)S(1)}, u32[]{:S(2)}, u32[]{:S(2)}) async-start(bf16[4,8,128,128]{3,2,1,0:T(8,128)(2,1)} %broadcast_select_fusion.3), calls=%async_computation.1 | async-start | bytes 2097152 | tf_op jit(solution)/shard_map/all_to_all | solution.py:50
  28.2 89.0 %all-gather.6.cloned.1.call-start = ((), (), s32[]{:S(2)}) async-start(), calls=%async_computation.3 | async-start | bytes 2621440 | tf_op jit(solution)/shard_map/all_gather | solution.py:61
Sparse Core Ops, SparseCore 0:
  17.3 24.0 all-gather.3
  95.5 21.7 all-gather.5
where the time goes:
time: 151 us
  waiting for transfers between devices  48.9 us (32%)
  local copies, waits for them, and re-layouts  34.6 us (23%)
  other arithmetic  26 us (17%)
  matrix products  17.9 us (12%)
  between operations  13.5 us (9%)
  starting transfers between devices  9.9 us (7%)
    all_gather x1, waiting for transfers between devices, per_device(): lax.all_gather(square_stored, 'col', axis=1, tiled=True)  21.9 us
    all_to_all x1, waiting for transfers between devices, per_device(): lax.all_to_all(reply, 'row', split_axis=0, concat_axis=0, tiled=True)  21.5 us
    gather x2, local copies, waits for them, and re-layouts, stacked_product(): jnp.take(left_panel, left_index.reshape(-1), axis=0)  20.6 us
    dot_general x2, matrix products, stacked_product(): jnp.einsum('stij,stjk->sik', left_stack, right_stack, preferred_element_t...  17.9 us
    select_n x3, other arithmetic, stacked_product(): jnp.take(left_panel, left_index.reshape(-1), axis=0)  14.9 us
    gather x1, local copies, waits for them, and re-layouts, stacked_product(): jnp.take(right_panel, right_index.reshape(-1), axis=0)  8.59 us
    select_n x1, other arithmetic, stacked_product(): jnp.take(right_panel, right_index.reshape(-1), axis=0)  7.42 us
    all_to_all x1, starting transfers between devices, per_device(): lax.all_to_all(request, 'row', split_axis=0, concat_axis=0, tiled=True)  6.32 us
  transfers between devices with their start and end apart: 4, of which 3 were waited for; matrix products, arithmetic and copies ran while one was open for 15% of the time, Pallas kernels for 0%

commit v1 on v0

v1 whole, which is shorter than its diff:
```python
import functools

import jax
import jax.numpy as jnp
from jax import lax
from jax.experimental import pallas as pl
from jax.experimental.pallas import tpu as pltpu
from jax.sharding import PartitionSpec as P

CAP = 8
LANES = 128
SMEM = pl.BlockSpec(memory_space=pltpu.SMEM)
VMEM = pl.BlockSpec(memory_space=pltpu.VMEM)


def params():
    return pltpu.CompilerParams(vmem_limit_bytes=48 * 1024 * 1024)


def cube_like(extent):
    return extent & (extent - 1) == 0


def prepare_kernel(slots, rows, cols, relative, pairs_ref, count_ref, table_ref, *request_refs):
    terms = pairs_ref.shape[2]
    row, col = lax.axis_index("row"), lax.axis_index("col")
    keys = rows * slots
    key = lax.broadcasted_iota(jnp.int32, (keys, terms), 0)
    source, slot = key // slots, key % slots
    if relative:
        wanted = ((row - source + rows) % rows) * slots + slot
    else:
        wanted = key
    used = jnp.zeros((keys, terms), jnp.int32)
    for s in range(slots):
        used = jnp.where(pairs_ref[s, 1:2, :] == wanted, 1, used)
    used = jnp.max(used, axis=1, keepdims=True)
    across = lax.broadcasted_iota(jnp.int32, (keys, keys), 1)
    down = lax.broadcasted_iota(jnp.int32, (keys, keys), 0)
    before = (across // slots == down // slots) & (across < down)
    rank = jnp.dot(
        before.astype(jnp.bfloat16),
        jnp.broadcast_to(used, (keys, LANES)).astype(jnp.bfloat16),
        preferred_element_type=jnp.float32,
    ).astype(jnp.int32)
    used = jnp.broadcast_to(used, (keys, LANES))
    lane = lax.broadcasted_iota(jnp.int32, (keys, LANES), 1)
    slot = lax.broadcasted_iota(jnp.int32, (keys, LANES), 0) % slots
    listed = jnp.where((used > 0) & (rank == lane), slot, 0)
    if relative:
        for distance, request_ref in enumerate(request_refs, 1):
            part = listed[distance * slots : (distance + 1) * slots]
            request_ref[...] = jnp.sum(part, axis=0, keepdims=True)
    else:
        request_refs[0][...] = jnp.sum(listed.reshape(rows, slots, LANES), axis=1)
    source, slot = key // slots, key % slots
    if relative:
        place = jnp.where(source == 0, slot, slots + (source - 1) * CAP + rank[:, :terms])
    else:
        place = jnp.where(source == row, slot, slots + source * CAP + rank[:, :terms])
    counts = count_ref[...]
    term = lax.broadcasted_iota(jnp.int32, (1, terms), 1)
    for s in range(slots):
        left = pairs_ref[s, 0:1, :]
        if cube_like(cols):
            left = ((left // slots) ^ col) * slots + left % slots
        active = term < counts[:, s : s + 1]
        table_ref[s : s + 1, :] = jnp.where(active, left, cols * slots)
        hit = pairs_ref[s, 1:2, :] == wanted
        table_ref[slots + s : slots + s + 1, :] = jnp.sum(
            jnp.where(hit, place, 0), axis=0, keepdims=True
        )


def pick_kernel(sets, *refs):
    asked_refs, blocks_ref, out_refs = refs[:sets], refs[sets], refs[sets + 1 :]
    for asked_ref, out_ref in zip(asked_refs, out_refs):
        for group in range(asked_ref.shape[0]):
            for place in range(CAP):
                out_ref[group * CAP + place] = blocks_ref[asked_ref[group, place]]


def fill(panel_ref, piece_refs):
    at = 0
    for piece_ref in piece_refs:
        count = piece_ref.shape[0]
        panel_ref[at : at + count] = piece_ref[...]
        at += count
    return at


def sum_products(table_ref, left_ref, right_ref, slots, terms, finish):
    def body(step, carry):
        for s in (2 * step, 2 * step + 1):
            left = jnp.concatenate([left_ref[table_ref[s, t]] for t in range(terms)], axis=1)
            right = jnp.concatenate(
                [right_ref[table_ref[slots + s, t]] for t in range(terms)], axis=0
            )
            finish(s, jnp.dot(left, right, preferred_element_type=jnp.float32))
        return carry

    lax.fori_loop(0, slots // 2, body, 0)


def square_kernel(lefts, table_ref, *refs):
    left_refs, right_refs = refs[:lefts], refs[lefts:-4]
    square_ref, stored_ref, left_ref, right_ref = refs[-4:]
    slots, terms = square_ref.shape[0], table_ref.shape[1]
    at = fill(left_ref, left_refs)
    left_ref[at] = jnp.zeros(left_ref.shape[1:], left_ref.dtype)
    fill(right_ref, right_refs)

    def finish(s, value):
        square_ref[s] = value
        stored_ref[s] = value.astype(jnp.bfloat16)

    sum_products(table_ref, left_ref, right_ref, slots, terms, finish)


def cube_kernel(lefts, table_ref, square_ref, *refs):
    left_refs, right_refs = refs[:lefts], refs[lefts:-3]
    out_ref, left_ref, right_ref = refs[-3:]
    slots, terms = square_ref.shape[0], table_ref.shape[1]
    at = fill(left_ref, left_refs)
    left_ref[at] = jnp.zeros(left_ref.shape[1:], left_ref.dtype)
    fill(right_ref, right_refs)

    def finish(s, value):
        out_ref[s] = (3.0 * square_ref[s] - 2.0 * value).astype(jnp.bfloat16)

    sum_products(table_ref, left_ref, right_ref, slots, terms, finish)


def row_panel(blocks, cols):
    if not cube_like(cols):
        return [lax.all_gather(blocks, "col", axis=0, tiled=True)]
    pieces = {0: blocks}
    bit = cols // 2
    while bit:
        for k in list(pieces):
            pieces[k ^ bit] = lax.ppermute(pieces[k], "col", [(i, i ^ bit) for i in range(cols)])
        bit //= 2
    return [pieces[k] for k in range(cols)]


def per_device(blocks, pairs, term_count):
    extent = blocks.shape[-1]
    slots, terms = pairs.shape[2], pairs.shape[3]
    rows, cols = lax.axis_size("row"), lax.axis_size("col")
    relative = rows <= 4
    local = blocks.reshape(slots, extent, extent)
    pairing = jnp.swapaxes(pairs.reshape(slots, terms, 2), 1, 2)
    request_shapes = [(1, LANES)] * (rows - 1) if relative else [(rows, LANES)]
    table, *requests = pl.pallas_call(
        functools.partial(prepare_kernel, slots, rows, cols, relative),
        out_shape=[jax.ShapeDtypeStruct((2 * slots, terms), jnp.int32)]
        + [jax.ShapeDtypeStruct(shape, jnp.int32) for shape in request_shapes],
        in_specs=[VMEM, VMEM],
        out_specs=[VMEM] * (1 + len(request_shapes)),
        compiler_params=params(),
    )(pairing, term_count.reshape(1, slots))
    if relative:
        asked = [
            lax.ppermute(request, "row", [(i, (i - d) % rows) for i in range(rows)])
            for d, request in enumerate(requests, 1)
        ]
    else:
        asked = [lax.all_to_all(requests[0], "row", split_axis=0, concat_axis=0, tiled=True)]
    picked = pl.pallas_call(
        functools.partial(pick_kernel, len(asked)),
        out_shape=[
            jax.ShapeDtypeStruct((a.shape[0] * CAP, extent, extent), blocks.dtype) for a in asked
        ],
        in_specs=[SMEM] * len(asked) + [VMEM],
        out_specs=[VMEM] * len(asked),
        compiler_params=params(),
    )(*asked, local)
    if relative:
        far = [
            lax.ppermute(piece, "row", [(i, (i + d) % rows) for i in range(rows)])
            for d, piece in enumerate(picked, 1)
        ]
    else:
        far = [lax.all_to_all(picked[0], "row", split_axis=0, concat_axis=0, tiled=True)]
    rights = [local, *far]
    right_count = sum(piece.shape[0] for piece in rights)
    scratch = [
        pltpu.VMEM((cols * slots + 1, extent, extent), blocks.dtype),
        pltpu.VMEM((right_count, extent, extent), blocks.dtype),
    ]
    whole = (slots, extent, extent)
    lefts = row_panel(local, cols)
    square, stored = pl.pallas_call(
        functools.partial(square_kernel, len(lefts)),
        out_shape=[
            jax.ShapeDtypeStruct(whole, jnp.float32),
            jax.ShapeDtypeStruct(whole, jnp.bfloat16),
        ],
        in_specs=[SMEM] + [VMEM] * (len(lefts) + len(rights)),
        out_specs=[VMEM, VMEM],
        scratch_shapes=scratch,
        compiler_params=params(),
    )(table, *lefts, *rights)
    lefts = row_panel(stored, cols)
    purified = pl.pallas_call(
        functools.partial(cube_kernel, len(lefts)),
        out_shape=jax.ShapeDtypeStruct(whole, jnp.bfloat16),
        in_specs=[SMEM] + [VMEM] * (1 + len(lefts) + len(rights)),
        out_specs=VMEM,
        scratch_shapes=scratch,
        compiler_params=params(),
    )(table, square, *lefts, *rights)
    return purified.reshape(blocks.shape)


def solution(mesh):
    placed = (
        P(("sys", "row"), "col", None, None, None),
        P(("sys", "row"), "col", None, None, None),
        P(("sys", "row"), "col", None),
    )
    return jax.shard_map(
        per_device,
        mesh=mesh,
        in_specs=placed,
        out_specs=P(("sys", "row"), "col", None, None, None),
        check_vma=False,
    )
```

time: 151 us -> 75.7 us (0.50)
  the two profiles are of different devices: /device:TPU:0 before, /device:TPU:9 now
where the time goes in v1:
time: 75.7 us; the launch traced here: 75.5 us
  waiting for transfers between devices  44.2 us (58%)
  starting transfers between devices  18.1 us (24%)
  Pallas kernels  10.7 us (14%)
  local copies, waits for them, and re-layouts  2.42 us (3%)
    ppermute x3, waiting for transfers between devices, per_device(): lax.ppermute(piece, 'row', [(i, (i + d) % rows) for i in range(rows)])  21.9 us
    ppermute x6, waiting for transfers between devices, row_panel(): lax.ppermute(pieces[k], 'col', [(i, i ^ bit) for i in range(cols)])  21.5 us
    ppermute x6, starting transfers between devices, row_panel(): lax.ppermute(pieces[k], 'col', [(i, i ^ bit) for i in range(cols)])  8.96 us
    pallas_call x1, Pallas kernels, per_device(): pl.pallas_call(functools.partial(cube_kernel, len(lefts)), out_shape=jax....  5.24 us
    ppermute x3, starting transfers between devices, per_device(): lax.ppermute(request, 'row', [(i, (i - d) % rows) for i in range(rows)])  4.72 us
    pallas_call x1, Pallas kernels, per_device(): pl.pallas_call(functools.partial(square_kernel, len(lefts)), out_shape=[j...  4.43 us
    ppermute x3, starting transfers between devices, per_device(): lax.ppermute(piece, 'row', [(i, (i + d) % rows) for i in range(rows)])  4.42 us
    unnamed x8, local copies, waits for them, and re-layouts  2.42 us
  transfers between devices with their start and end apart: 12, of which 7 were waited for; matrix products, arithmetic and copies ran while one was open for 0% of the time, Pallas kernels for 1%

profile of v1, /device:TPU:9, one launch (start us, length us, event | category | flops | bytes accessed | tf_op | source)
XLA Modules:
  0.0 75.5 jit_solution(16211562726959563060)
XLA Ops:
  0.0 1.2 %collective-permute-start.1 = (bf16[16,128,128]{2,1,0:T(8,128)(2,1)}, bf16[16,128,128]{2,1,0:T(8,128)(2,1)S(1)}, u32[]{:S(2)}, u32[]{:S(2)}) collective-permute-start(bf16[16,128,128]{2,1,0:T(8,128)(2,1)} %bitcast.6), channel_id=1, source_target_pairs={{0,2},{1,3},{2,0},{3,1},{4,6},{5,7},{6,4},{7,5},{8,10},{9,11},{10,... | collective-permute-start | bytes 1572872 | tf_op jit(solution)/shard_map/ppermute | solution.py:141
  1.2 1.0 %collective-permute-start = (bf16[16,128,128]{2,1,0:T(8,128)(2,1)}, bf16[16,128,128]{2,1,0:T(8,128)(2,1)S(1)}, u32[]{:S(2)}, u32[]{:S(2)}) collective-permute-start(bf16[16,128,128]{2,1,0:T(8,128)(2,1)} %bitcast.7), channel_id=1, source_target_pairs={{0,1},{1,0},{2,3},{3,2},{4,5},{5,4},{6,7},{7,6},{8,9},{9,8},{10,11... | collective-permute-start | bytes 1572872 | tf_op jit(solution)/shard_map/ppermute | solution.py:141
  2.2 10.8 %collective-permute-done.1.refs_2_ = bf16[16,128,128]{2,1,0:T(8,128)(2,1)S(1)} collective-permute-done((bf16[16,128,128]{2,1,0:T(8,128)(2,1)}, bf16[16,128,128]{2,1,0:T(8,128)(2,1)S(1)}, u32[]{:S(2)}, u32[]{:S(2)}) %collective-permute-start.1) | collective-permute-done | bytes 524320 | tf_op jit(solution)/shard_map/ppermute | solution.py:141
  13.0 1.5 %collective-permute-start.2 = (bf16[16,128,128]{2,1,0:T(8,128)(2,1)S(1)}, bf16[16,128,128]{2,1,0:T(8,128)(2,1)S(1)}, u32[]{:S(2)}, u32[]{:S(2)}) collective-permute-start(bf16[16,128,128]{2,1,0:T(8,128)(2,1)S(1)} %collective-permute-done.1.refs_2_), channel_id=1, source_target_pairs={{0,1},{1,0},{2,3},{3,2},{4,5},{5,4},{6,7},{7,6},{8,9},{9,8},{10,11... | collective-permute-start | bytes 1572872 | tf_op jit(solution)/shard_map/ppermute | solution.py:141
  14.6 0.7 copy-done.3
  15.2 0.7 copy-done.2
  15.9 0.5 shard_map.37
  16.4 0.1 collective-permute-start.3
  16.5 2.5 %collective-permute-start.4 = (s32[1,128]{1,0:T(1,128)S(1)}, s32[1,128]{1,0:T(1,128)S(1)}, u32[]{:S(2)}, u32[]{:S(2)}) collective-permute-start(s32[1,128]{1,0:T(1,128)S(1)} %get-tuple-element.16), channel_id=1, source_target_pairs={{0,8},{4,12},{8,0},{12,4},{1,9},{5,13},{9,1},{13,5},{2,10},{6,14},... | collective-permute-start | bytes 1544 | tf_op jit(solution)/shard_map/ppermute | solution.py:164
  18.9 2.2 %collective-permute-start.5 = (s32[1,128]{1,0:T(1,128)S(1)}, s32[1,128]{1,0:T(1,128)S(1)}, u32[]{:S(2)}, u32[]{:S(2)}) collective-permute-start(s32[1,128]{1,0:T(1,128)S(1)} %get-tuple-element.17), channel_id=1, source_target_pairs={{0,4},{4,8},{8,12},{12,0},{1,5},{5,9},{9,13},{13,1},{2,6},{6,10},{... | collective-permute-start | bytes 1544 | tf_op jit(solution)/shard_map/ppermute | solution.py:164
  21.1 0.0 collective-permute-done.3.refs_0_
  21.1 0.0 collective-permute-done.4.refs_1_
  21.1 0.7 collective-permute-done.5.refs_2_
  21.8 1.0 %copy-done = bf16[1,1,16,128,128]{4,3,2,1,0:T(8,128)(2,1)S(1)} copy-done((bf16[1,1,16,128,128]{4,3,2,1,0:T(8,128)(2,1)S(1)}, bf16[1,1,16,128,128]{4,3,2,1,0:T(8,128)(2,1)}, u32[]{:S(2)}) %copy-start) | copy-done | bytes 524312
  22.9 0.6 shard_map.38
  23.5 1.7 %collective-permute-start.6 = (bf16[8,128,128]{2,1,0:T(8,128)(2,1)S(1)}, bf16[8,128,128]{2,1,0:T(8,128)(2,1)S(1)}, u32[]{:S(2)}, u32[]{:S(2)}) collective-permute-start(bf16[8,128,128]{2,1,0:T(8,128)(2,1)S(1)} %get-tuple-element.18), channel_id=1, source_target_pairs={{0,4},{4,8},{8,12},{12,0},{1,5},{5,9},{9,13},{13,1},{2,6},{6,10},{... | collective-permute-start | bytes 786440 | tf_op jit(solution)/shard_map/ppermute | solution.py:180
  25.2 2.7 %collective-permute-start.7 = (bf16[8,128,128]{2,1,0:T(8,128)(2,1)S(1)}, bf16[8,128,128]{2,1,0:T(8,128)(2,1)S(1)}, u32[]{:S(2)}, u32[]{:S(2)}) collective-permute-start(bf16[8,128,128]{2,1,0:T(8,128)(2,1)S(1)} %get-tuple-element.19), channel_id=1, source_target_pairs={{0,8},{4,12},{8,0},{12,4},{1,9},{5,13},{9,1},{13,5},{2,10},{6,14},... | collective-permute-start | bytes 786440 | tf_op jit(solution)/shard_map/ppermute | solution.py:180
  27.9 0.0 collective-permute-start.8
  27.9 3.1 %collective-permute-done.6.refs_5_ = bf16[8,128,128]{2,1,0:T(8,128)(2,1)S(1)} collective-permute-done((bf16[8,128,128]{2,1,0:T(8,128)(2,1)S(1)}, bf16[8,128,128]{2,1,0:T(8,128)(2,1)S(1)}, u32[]{:S(2)}, u32[]{:S(2)}) %collective-permute-start.6) | collective-permute-done | bytes 262176 | tf_op jit(solution)/shard_map/ppermute | solution.py:180
  31.0 14.9 %collective-permute-done.7.refs_6_ = bf16[8,128,128]{2,1,0:T(8,128)(2,1)S(1)} collective-permute-done((bf16[8,128,128]{2,1,0:T(8,128)(2,1)S(1)}, bf16[8,128,128]{2,1,0:T(8,128)(2,1)S(1)}, u32[]{:S(2)}, u32[]{:S(2)}) %collective-permute-start.7) | collective-permute-done | bytes 262176 | tf_op jit(solution)/shard_map/ppermute | solution.py:180
  46.0 3.9 %collective-permute-done.8.refs_7_ = bf16[8,128,128]{2,1,0:T(8,128)(2,1)S(1)} collective-permute-done((bf16[8,128,128]{2,1,0:T(8,128)(2,1)S(1)}, bf16[8,128,128]{2,1,0:T(8,128)(2,1)S(1)}, u32[]{:S(2)}, u32[]{:S(2)}) %collective-permute-start.8) | collective-permute-done | bytes 262176 | tf_op jit(solution)/shard_map/ppermute | solution.py:180
  49.9 0.0 collective-permute-done.refs_1_
  49.9 0.0 collective-permute-done.2.refs_3_
  49.9 0.0 copy-done.1
  49.9 4.4 %shard_map.39 = (f32[16,128,128]{2,1,0:T(8,128)S(1)}, bf16[16,128,128]{2,1,0:T(8,128)(2,1)S(1)}) custom-call(s32[32,16]{1,0:T(8,128)S(1)} %get-tuple-element.14.table_ref, bf16[16,128,128]{2,1,0:T(8,128)(2,1)S(1)} %bitcast.9, bf16[16,128,128]{2,1,0:T(8,128)(2,1)S(1)} %collective-permute-done.refs_1_, ...), custom_call_target="tpu_custom_call" | custom-call | tf_op jit(solution)/shard_map/pallas_call | solution.py:193
  54.3 1.3 %collective-permute-start.10 = (bf16[16,128,128]{2,1,0:T(8,128)(2,1)S(1)}, bf16[16,128,128]{2,1,0:T(8,128)(2,1)S(1)}, u32[]{:S(2)}, u32[]{:S(2)}) collective-permute-start(bf16[16,128,128]{2,1,0:T(8,128)(2,1)S(1)} %get-tuple-element.22.refs_0_), channel_id=1, source_target_pairs={{0,2},{1,3},{2,0},{3,1},{4,6},{5,7},{6,4},{7,5},{8,10},{9,11},{10,... | collective-permute-start | bytes 1572872 | tf_op jit(solution)/shard_map/ppermute | solution.py:141
  55.6 1.7 %collective-permute-start.9 = (bf16[16,128,128]{2,1,0:T(8,128)(2,1)S(1)}, bf16[16,128,128]{2,1,0:T(8,128)(2,1)S(1)}, u32[]{:S(2)}, u32[]{:S(2)}) collective-permute-start(bf16[16,128,128]{2,1,0:T(8,128)(2,1)S(1)} %get-tuple-element.22.refs_0_), channel_id=1, source_target_pairs={{0,1},{1,0},{2,3},{3,2},{4,5},{5,4},{6,7},{7,6},{8,9},{9,8},{10,11... | collective-permute-start | bytes 1572872 | tf_op jit(solution)/shard_map/ppermute | solution.py:141
  57.3 9.2 %collective-permute-done.10.refs_2_ = bf16[16,128,128]{2,1,0:T(8,128)(2,1)S(1)} collective-permute-done((bf16[16,128,128]{2,1,0:T(8,128)(2,1)S(1)}, bf16[16,128,128]{2,1,0:T(8,128)(2,1)S(1)}, u32[]{:S(2)}, u32[]{:S(2)}) %collective-permute-start.10) | collective-permute-done | bytes 524320 | tf_op jit(solution)/shard_map/ppermute | solution.py:141
  66.4 2.3 %collective-permute-start.11 = (bf16[16,128,128]{2,1,0:T(8,128)(2,1)S(1)}, bf16[16,128,128]{2,1,0:T(8,128)(2,1)S(1)}, u32[]{:S(2)}, u32[]{:S(2)}) collective-permute-start(bf16[16,128,128]{2,1,0:T(8,128)(2,1)S(1)} %collective-permute-done.10.refs_2_), channel_id=1, source_target_pairs={{0,1},{1,0},{2,3},{3,2},{4,5},{5,4},{6,7},{7,6},{8,9},{9,8},{10,11... | collective-permute-start | bytes 1572872 | tf_op jit(solution)/shard_map/ppermute | solution.py:141
  68.7 0.0 collective-permute-done.9.refs_1_
  68.7 1.5 %collective-permute-done.11.refs_3_ = bf16[16,128,128]{2,1,0:T(8,128)(2,1)S(1)} collective-permute-done((bf16[16,128,128]{2,1,0:T(8,128)(2,1)S(1)}, bf16[16,128,128]{2,1,0:T(8,128)(2,1)S(1)}, u32[]{:S(2)}, u32[]{:S(2)}) %collective-permute-start.11) | collective-permute-done | bytes 524320 | tf_op jit(solution)/shard_map/ppermute | solution.py:141
  70.3 5.2 %shard_map.40 = bf16[16,128,128]{2,1,0:T(8,128)(2,1)} custom-call(s32[32,16]{1,0:T(8,128)S(1)} %get-tuple-element.14.table_ref, f32[16,128,128]{2,1,0:T(8,128)S(1)} %get-tuple-element.21.square_ref, bf16[16,128,128]{2,1,0:T(8,128)(2,1)S(1)} %get-tuple-element.22.refs_0_, bf16[16,128,128]{2,1,0:T(8,128)(2,1)S(1)} %collective-permute-done.9.refs_1_, ...), custom_call_target="tpu_custom_call" | custom-call | tf_op jit(solution)/shard_map/pallas_call | solution.py:205
  (4 shorter events, 0.0 us)
Async XLA Ops:
  0.0 13.0 %collective-permute-start.1 = (bf16[16,128,128]{2,1,0:T(8,128)(2,1)}, bf16[16,128,128]{2,1,0:T(8,128)(2,1)S(1)}, u32[]{:S(2)}, u32[]{:S(2)}) collective-permute-start(bf16[16,128,128]{2,1,0:T(8,128)(2,1)} %bitcast.6), channel_id=1, source_target_pairs={{0,2},{1,3},{2,0},{3,1},{4,6},{5,7},{6,4},{7,5},{8,10},{9,11},{10,... | collective-permute-start | bytes 1572872 | tf_op jit(solution)/shard_map/ppermute | solution.py:141
  1.2 48.7 %collective-permute-start = (bf16[16,128,128]{2,1,0:T(8,128)(2,1)}, bf16[16,128,128]{2,1,0:T(8,128)(2,1)S(1)}, u32[]{:S(2)}, u32[]{:S(2)}) collective-permute-start(bf16[16,128,128]{2,1,0:T(8,128)(2,1)} %bitcast.7), channel_id=1, source_target_pairs={{0,1},{1,0},{2,3},{3,2},{4,5},{5,4},{6,7},{7,6},{8,9},{9,8},{10,11... | collective-permute-start | bytes 1572872 | tf_op jit(solution)/shard_map/ppermute | solution.py:141
  13.0 36.9 %collective-permute-start.2 = (bf16[16,128,128]{2,1,0:T(8,128)(2,1)S(1)}, bf16[16,128,128]{2,1,0:T(8,128)(2,1)S(1)}, u32[]{:S(2)}, u32[]{:S(2)}) collective-permute-start(bf16[16,128,128]{2,1,0:T(8,128)(2,1)S(1)} %collective-permute-done.1.refs_2_), channel_id=1, source_target_pairs={{0,1},{1,0},{2,3},{3,2},{4,5},{5,4},{6,7},{7,6},{8,9},{9,8},{10,11... | collective-permute-start | bytes 1572872 | tf_op jit(solution)/shard_map/ppermute | solution.py:141
  14.6 0.7 copy-start.3
  15.2 0.7 copy-start.2
  16.4 4.7 %collective-permute-start.3 = (s32[1,128]{1,0:T(1,128)S(1)}, s32[1,128]{1,0:T(1,128)S(1)}, u32[]{:S(2)}, u32[]{:S(2)}) collective-permute-start(s32[1,128]{1,0:T(1,128)S(1)} %get-tuple-element.15), channel_id=1, source_target_pairs={{0,12},{4,0},{8,4},{12,8},{1,13},{5,1},{9,5},{13,9},{2,14},{6,2},{... | collective-permute-start | bytes 1544 | tf_op jit(solution)/shard_map/ppermute | solution.py:164
  16.5 4.7 %collective-permute-start.4 = (s32[1,128]{1,0:T(1,128)S(1)}, s32[1,128]{1,0:T(1,128)S(1)}, u32[]{:S(2)}, u32[]{:S(2)}) collective-permute-start(s32[1,128]{1,0:T(1,128)S(1)} %get-tuple-element.16), channel_id=1, source_target_pairs={{0,8},{4,12},{8,0},{12,4},{1,9},{5,13},{9,1},{13,5},{2,10},{6,14},... | collective-permute-start | bytes 1544 | tf_op jit(solution)/shard_map/ppermute | solution.py:164
  18.9 2.9 %collective-permute-start.5 = (s32[1,128]{1,0:T(1,128)S(1)}, s32[1,128]{1,0:T(1,128)S(1)}, u32[]{:S(2)}, u32[]{:S(2)}) collective-permute-start(s32[1,128]{1,0:T(1,128)S(1)} %get-tuple-element.17), channel_id=1, source_target_pairs={{0,4},{4,8},{8,12},{12,0},{1,5},{5,9},{9,13},{13,1},{2,6},{6,10},{... | collective-permute-start | bytes 1544 | tf_op jit(solution)/shard_map/ppermute | solution.py:164
  21.8 1.0 %copy-start = (bf16[1,1,16,128,128]{4,3,2,1,0:T(8,128)(2,1)S(1)}, bf16[1,1,16,128,128]{4,3,2,1,0:T(8,128)(2,1)}, u32[]{:S(2)}) copy-start(bf16[1,1,16,128,128]{4,3,2,1,0:T(8,128)(2,1)} %param.3) | copy-start | bytes 1572868
  22.9 27.0 %copy-start.1 = (bf16[1,1,16,128,128]{4,3,2,1,0:T(8,128)(2,1)S(1)}, bf16[1,1,16,128,128]{4,3,2,1,0:T(8,128)(2,1)}, u32[]{:S(2)}) copy-start(bf16[1,1,16,128,128]{4,3,2,1,0:T(8,128)(2,1)} %param.3) | copy-start | bytes 1572868
  23.5 7.5 %collective-permute-start.6 = (bf16[8,128,128]{2,1,0:T(8,128)(2,1)S(1)}, bf16[8,128,128]{2,1,0:T(8,128)(2,1)S(1)}, u32[]{:S(2)}, u32[]{:S(2)}) collective-permute-start(bf16[8,128,128]{2,1,0:T(8,128)(2,1)S(1)} %get-tuple-element.18), channel_id=1, source_target_pairs={{0,4},{4,8},{8,12},{12,0},{1,5},{5,9},{9,13},{13,1},{2,6},{6,10},{... | collective-permute-start | bytes 786440 | tf_op jit(solution)/shard_map/ppermute | solution.py:180
  25.2 20.7 %collective-permute-start.7 = (bf16[8,128,128]{2,1,0:T(8,128)(2,1)S(1)}, bf16[8,128,128]{2,1,0:T(8,128)(2,1)S(1)}, u32[]{:S(2)}, u32[]{:S(2)}) collective-permute-start(bf16[8,128,128]{2,1,0:T(8,128)(2,1)S(1)} %get-tuple-element.19), channel_id=1, source_target_pairs={{0,8},{4,12},{8,0},{12,4},{1,9},{5,13},{9,1},{13,5},{2,10},{6,14},... | collective-permute-start | bytes 786440 | tf_op jit(solution)/shard_map/ppermute | solution.py:180
  27.9 21.9 %collective-permute-start.8 = (bf16[8,128,128]{2,1,0:T(8,128)(2,1)S(1)}, bf16[8,128,128]{2,1,0:T(8,128)(2,1)S(1)}, u32[]{:S(2)}, u32[]{:S(2)}) collective-permute-start(bf16[8,128,128]{2,1,0:T(8,128)(2,1)S(1)} %get-tuple-element.20), channel_id=1, source_target_pairs={{0,12},{4,0},{8,4},{12,8},{1,13},{5,1},{9,5},{13,9},{2,14},{6,2},{... | collective-permute-start | bytes 786440 | tf_op jit(solution)/shard_map/ppermute | solution.py:180
  54.3 12.1 %collective-permute-start.10 = (bf16[16,128,128]{2,1,0:T(8,128)(2,1)S(1)}, bf16[16,128,128]{2,1,0:T(8,128)(2,1)S(1)}, u32[]{:S(2)}, u32[]{:S(2)}) collective-permute-start(bf16[16,128,128]{2,1,0:T(8,128)(2,1)S(1)} %get-tuple-element.22.refs_0_), channel_id=1, source_target_pairs={{0,2},{1,3},{2,0},{3,1},{4,6},{5,7},{6,4},{7,5},{8,10},{9,11},{10,... | collective-permute-start | bytes 1572872 | tf_op jit(solution)/shard_map/ppermute | solution.py:141
  55.6 13.1 %collective-permute-start.9 = (bf16[16,128,128]{2,1,0:T(8,128)(2,1)S(1)}, bf16[16,128,128]{2,1,0:T(8,128)(2,1)S(1)}, u32[]{:S(2)}, u32[]{:S(2)}) collective-permute-start(bf16[16,128,128]{2,1,0:T(8,128)(2,1)S(1)} %get-tuple-element.22.refs_0_), channel_id=1, source_target_pairs={{0,1},{1,0},{2,3},{3,2},{4,5},{5,4},{6,7},{7,6},{8,9},{9,8},{10,11... | collective-permute-start | bytes 1572872 | tf_op jit(solution)/shard_map/ppermute | solution.py:141
  66.4 3.8 %collective-permute-start.11 = (bf16[16,128,128]{2,1,0:T(8,128)(2,1)S(1)}, bf16[16,128,128]{2,1,0:T(8,128)(2,1)S(1)}, u32[]{:S(2)}, u32[]{:S(2)}) collective-permute-start(bf16[16,128,128]{2,1,0:T(8,128)(2,1)S(1)} %collective-permute-done.10.refs_2_), channel_id=1, source_target_pairs={{0,1},{1,0},{2,3},{3,2},{4,5},{5,4},{6,7},{7,6},{8,9},{9,8},{10,11... | collective-permute-start | bytes 1572872 | tf_op jit(solution)/shard_map/ppermute | solution.py:141

commit v2 on v0

v2 whole, which is shorter than its diff:
```python
import functools
import math

import jax
import jax.numpy as jnp
from jax import lax
from jax.experimental import pallas as pl
from jax.experimental.pallas import tpu as pltpu
from jax.sharding import PartitionSpec as P

CAP = 8
LANES = 128
MIB = 1 << 20
CHUNK = 16
FIELD = 1024
SMEM = pl.BlockSpec(memory_space=pltpu.SMEM)
VMEM = pl.BlockSpec(memory_space=pltpu.VMEM)


def params(limit):
    return pltpu.CompilerParams(vmem_limit_bytes=limit)


def cost(us):
    return pl.CostEstimate(
        flops=int(us * 10**9) + 10**5, bytes_accessed=int(us * 3 * 10**6) + 10**3, transcendentals=0
    )


def is_power(extent):
    return extent & (extent - 1) == 0


def prepare_kernel(slots, rows, cols, line, pairs_ref, table_ref, request_ref):
    terms = pairs_ref.shape[2]
    row, col = lax.axis_index("row"), lax.axis_index("col")
    keys = rows * slots
    key = lax.broadcasted_iota(jnp.int32, (keys, terms), 0)
    used = jnp.zeros((keys, terms), jnp.int32)
    for s in range(slots):
        used = jnp.where(pairs_ref[s, 1:2, :] == key, 1, used)
    used = jnp.max(used, axis=1, keepdims=True)
    across = lax.broadcasted_iota(jnp.int32, (keys, keys), 1)
    down = lax.broadcasted_iota(jnp.int32, (keys, keys), 0)
    before = (across // slots == down // slots) & (across < down)
    used = jnp.broadcast_to(used, (keys, LANES))
    rank = jnp.dot(
        before.astype(jnp.bfloat16),
        used.astype(jnp.bfloat16),
        preferred_element_type=jnp.float32,
    ).astype(jnp.int32)
    lane = lax.broadcasted_iota(jnp.int32, (keys, LANES), 1)
    place = lax.broadcasted_iota(jnp.int32, (keys, LANES), 0)
    listed = jnp.where((used > 0) & (rank == lane), place % slots, 0)
    source, slot, rank = key // slots, key % slots, rank[:, :terms]
    if line:
        far = jnp.abs(place // slots - row)
        for distance in (2, 3):
            part = jnp.where(far == distance, listed, 0)
            request_ref[distance - 2 : distance - 1, :] = jnp.sum(part, axis=0, keepdims=True)
        away = jnp.abs(source - row)
        is_end = (row == 0) | (row == rows - 1)
        place = jnp.where(away == 0, slot, 2 * slots + slot)
        place = jnp.where(source == row ^ 1, slots + slot, place)
        place = jnp.where(away == 2, 3 * slots + jnp.where(is_end, rank, slot), place)
        place = jnp.where(away == 3, 3 * slots + CAP + rank, place)
    else:
        request_ref[...] = jnp.sum(listed.reshape(rows, slots, LANES), axis=1)
        place = jnp.where(source == row, slot, slots + source * CAP + rank)
    for s in range(slots):
        left = pairs_ref[s, 0:1, :]
        if is_power(cols):
            left = ((left // slots) ^ col) * slots + left % slots
        hit = pairs_ref[s, 1:2, :] == key
        right = jnp.sum(jnp.where(hit, place, 0), axis=0, keepdims=True)
        table_ref[s : s + 1, :] = left + FIELD * (right + FIELD * s)


def plan_kernel(near, close, blank, table_ref, count_ref, plan_ref, total_ref):
    slots = table_ref.shape[0]
    room = plan_ref.shape[0] // 4

    def blank_of(s):
        return blank + FIELD * FIELD * s

    def block(s, ends):
        def term(t, ends):
            word = table_ref[s, t]
            is_near = ((word // FIELD) % FIELD < near).astype(jnp.int32)
            is_close = (word % FIELD < close).astype(jnp.int32)
            for end in ends:
                plan_ref[end] = word
            a, b, c, d = ends
            return a + is_near, b + 1 - is_near, c + is_close, d + 1 - is_close

        ends = lax.fori_loop(0, count_ref[0, s], term, ends)
        for end in ends:
            plan_ref[end] = blank_of(s)
        return tuple(end + end % 2 for end in ends)

    ends = lax.fori_loop(0, slots, block, tuple(jnp.int32(i * room) for i in range(4)))
    for i, end in enumerate(ends):
        total_ref[i] = end - i * room

        def pad(j, carry, end=end):
            plan_ref[end + j] = blank
            return carry

        lax.fori_loop(0, 2 * CHUNK, pad, 0)


def halves(first, second):
    half = first.shape[-1] // 2
    return (
        jnp.concatenate([first[:, :half], second[:, :half]], axis=1),
        jnp.concatenate([first[:, half:], second[:, half:]], axis=1),
    )


def pick(asked_ref, group, source_ref, left_ref, right_ref):
    for p in range(CAP // 2):
        first = source_ref[asked_ref[group, 2 * p]]
        second = source_ref[asked_ref[group, 2 * p + 1]]
        at = group * (CAP // 2) + p
        left_ref[at], right_ref[at] = halves(first, second)


def pick_far_kernel(asked_ref, blocks_ref, left_ref, right_ref):
    for group in range(asked_ref.shape[0]):
        pick(asked_ref, group, blocks_ref, left_ref, right_ref)


def relay_kernel(after_ref, partner_ref, low_ref, high_ref):
    row = lax.axis_index("row")

    @pl.when((row == 1) | (row == 2))
    def _():
        for p in range(low_ref.shape[0]):
            low_ref[p], high_ref[p] = halves(partner_ref[2 * p], partner_ref[2 * p + 1])


def early_kernel(asked_ref, middle_ref, out_ref):
    row = lax.axis_index("row")

    @pl.when((row == 1) | (row == 2))
    def _():
        pick(asked_ref, 0, middle_ref, out_ref, out_ref.at[CAP // 2 :])


def late_kernel(asked_ref, passed_ref, after_ref, out_ref):
    row = lax.axis_index("row")
    half = passed_ref.shape[-1] // 2

    def side(place):
        slot = asked_ref[1, place]
        both = passed_ref[slot // 2]
        return jnp.where(slot % 2 == 0, both, turned(both))[:, :half]

    @pl.when((row == 1) | (row == 2))
    def _():
        for p in range(CAP // 2):
            out_ref[p] = jnp.concatenate([side(2 * p), side(2 * p + 1)], axis=1)


def fill(panel_ref, piece_refs):
    at = 0
    for piece_ref in piece_refs:
        count = piece_ref.shape[0]
        panel_ref[at : at + count] = piece_ref[...]
        at += count
    return at


def turned(block):
    half = block.shape[-1] // 2
    return jnp.concatenate([block[:, half:], block[:, :half]], axis=1)


def add_products(plan_ref, total_ref, which, left_ref, right_ref, sum_ref, left_shift=0):
    room = plan_ref.shape[0] // 4

    def step(c, carry):
        for p in range(CHUNK):
            first = plan_ref[which * room + 2 * (c * CHUNK + p)]
            second = plan_ref[which * room + 2 * (c * CHUNK + p) + 1]
            left = jnp.concatenate(
                [left_ref[word % FIELD - left_shift] for word in (first, second)], axis=1
            )
            right = jnp.concatenate(
                [right_ref[(word // FIELD) % FIELD] for word in (first, second)], axis=0
            )
            sum_ref[first // (FIELD * FIELD)] += jnp.dot(
                left, right, preferred_element_type=jnp.float32
            )
        return carry

    lax.fori_loop(0, (total_ref[which] + 2 * CHUNK - 1) // (2 * CHUNK), step, 0)


def near_kernel(lefts, plan_ref, total_ref, *refs):
    left_refs, right_refs = refs[:lefts], refs[lefts:-4]
    sum_ref, left_ref, token_ref, right_ref = refs[-4:]
    token_ref[...] = jnp.zeros(token_ref.shape, token_ref.dtype)
    at = fill(left_ref, left_refs)
    left_ref[at] = jnp.zeros(left_ref.shape[1:], left_ref.dtype)
    fill(right_ref, right_refs)
    sum_ref[...] = jnp.zeros(sum_ref.shape, sum_ref.dtype)
    add_products(plan_ref, total_ref, 0, left_ref, right_ref, sum_ref)


def unpack(panel_ref, at, piece_ref, first, count):
    for p in range(count):
        both = piece_ref[first + p]
        panel_ref[at + 2 * p] = both
        panel_ref[at + 2 * p + 1] = turned(both)


def far_kernel(start, turn, line, plan_ref, total_ref, near_ref, left_ref, after_ref, *refs):
    far_refs = refs[:-3]
    sum_ref, stored_ref, right_ref = refs[-3:]
    right_ref[0] = jnp.zeros(right_ref.shape[1:], right_ref.dtype)
    if line:
        row = lax.axis_index("row")

        @pl.when((row == 1) | (row == 2))
        def _():
            unpack(right_ref, start, far_refs[0], 0, far_refs[0].shape[0])

        @pl.when((row == 0) | (row == 3))
        def _():
            unpack(right_ref, start, far_refs[1], turn * CAP // 2, CAP // 2)
            unpack(right_ref, start + CAP, far_refs[2], 0, CAP // 2)
    else:
        unpack(right_ref, start, far_refs[0], 0, far_refs[0].shape[0])
    for s in range(sum_ref.shape[0]):
        sum_ref[s] = turned(near_ref[s]) if turn else near_ref[s]
    add_products(plan_ref, total_ref, 1, left_ref, right_ref, sum_ref)
    half = sum_ref.shape[-1] // 2
    for p in range(stored_ref.shape[0]):
        both = [sum_ref[2 * p][:, :half], sum_ref[2 * p + 1][:, :half]]
        stored_ref[p] = jnp.concatenate(both, axis=1).astype(jnp.bfloat16)


def join(panel_ref, at, low_ref, high_ref, first, second, count):
    for p in range(count):
        panel_ref[at + 2 * p], panel_ref[at + 2 * p + 1] = halves(
            low_ref[first + p], high_ref[second + p]
        )


def close_kernel(closes, nears, line, blank, plan_ref, total_ref, after_ref, *refs):
    refs, (sum_ref, right_ref, token_ref, left_ref) = refs[:-4], refs[-4:]
    sums, refs = refs[:2], refs[2:]
    lows, highs, refs = refs[:closes], refs[closes : 2 * closes], refs[2 * closes :]
    near_refs, refs = refs[:nears], refs[nears:]
    token_ref[...] = jnp.zeros(token_ref.shape, token_ref.dtype)
    at = 0
    for low_ref, high_ref in zip(lows, highs):
        join(left_ref, at, low_ref, high_ref, 0, 0, low_ref.shape[0])
        at += 2 * low_ref.shape[0]
    left_ref[blank] = jnp.zeros(left_ref.shape[1:], left_ref.dtype)
    at = fill(right_ref, near_refs)
    if line:
        passed_low_ref, passed_high_ref, early_ref, late_low_ref, late_high_ref = refs
        row = lax.axis_index("row")

        @pl.when((row == 1) | (row == 2))
        def _():
            join(right_ref, at, passed_low_ref, passed_high_ref, 0, 0, passed_low_ref.shape[0])

        @pl.when((row == 0) | (row == 3))
        def _():
            join(right_ref, at, early_ref, early_ref, 0, CAP // 2, CAP // 2)
            join(right_ref, at + CAP, late_low_ref, late_high_ref, 0, 0, CAP // 2)
    else:
        join(right_ref, at, refs[0], refs[1], 0, 0, refs[0].shape[0])
    half = sum_ref.shape[-1] // 2
    for s in range(sum_ref.shape[0]):
        both = [sums[0][s][:, :half], sums[1][s][:, :half]]
        sum_ref[s] = -1.5 * jnp.concatenate(both, axis=1)
    add_products(plan_ref, total_ref, 2, left_ref, right_ref, sum_ref)


def distant_kernel(distants, close, plan_ref, total_ref, close_ref, right_ref, *refs):
    lows, highs = refs[:distants], refs[distants : 2 * distants]
    out_ref, left_ref, sum_ref = refs[-3:]
    at = 0
    for low_ref, high_ref in zip(lows, highs):
        join(left_ref, at, low_ref, high_ref, 0, 0, low_ref.shape[0])
        at += 2 * low_ref.shape[0]
    left_ref[at] = jnp.zeros(left_ref.shape[1:], left_ref.dtype)
    sum_ref[...] = close_ref[...]
    add_products(plan_ref, total_ref, 3, left_ref, right_ref, sum_ref, close)
    out_ref[...] = (-2.0 * sum_ref[...]).astype(jnp.bfloat16)


def nothing_kernel(value_ref, after_ref, out_ref):
    pass


def after(value, earlier, us=0):
    return pl.pallas_call(
        nothing_kernel,
        out_shape=jax.ShapeDtypeStruct(value.shape, value.dtype),
        in_specs=[VMEM, VMEM],
        out_specs=VMEM,
        input_output_aliases={0: 0},
        compiler_params=params(8 * MIB),
        cost_estimate=cost(us),
    )(value, earlier)


def row_panel(blocks, cols, earlier=None):
    if not is_power(cols):
        return [lax.all_gather(blocks, "col", axis=0, tiled=True)]
    pieces = spread(blocks, cols // 2, cols)
    if cols > 1:
        piece = cross(blocks, cols)
        if earlier is not None:
            piece = after(piece, earlier)
        pieces += spread(piece, cols // 2, cols)
    return pieces


def cross(blocks, cols):
    return lax.ppermute(blocks, "col", [(i, i ^ (cols // 2)) for i in range(cols)])


def per_device(blocks, pairs, term_count):
    extent = blocks.shape[-1]
    slots, terms = pairs.shape[2], pairs.shape[3]
    rows, cols = lax.axis_size("row"), lax.axis_size("col")
    line = rows == 4
    local = blocks.reshape(slots, extent, extent)
    pairing = jnp.swapaxes(pairs.reshape(slots, terms, 2), 1, 2)

    def call(kernel, outs, ins, scratch=(), smem=0, out_smem=False, us=2):
        sizes = [(a.shape, a.dtype) for a in ins[smem:]] + [(a.shape, a.dtype) for a in scratch]
        sizes += [] if out_smem else outs
        vmem = 4 * MIB + sum(math.prod(shape) * jnp.dtype(dtype).itemsize for shape, dtype in sizes)
        return pl.pallas_call(
            kernel,
            out_shape=[jax.ShapeDtypeStruct(shape, dtype) for shape, dtype in outs],
            in_specs=[SMEM] * smem + [VMEM] * (len(ins) - smem),
            out_specs=[SMEM if out_smem else VMEM] * len(outs),
            scratch_shapes=list(scratch),
            compiler_params=params(vmem),
            cost_estimate=cost(us),
        )(*ins)

    def blocks_of(count):
        return ((count, extent, extent), local.dtype)

    whole = ((slots, extent, extent), jnp.float32)
    requests = ((2 if line else rows, LANES), jnp.int32)
    table, request = call(
        functools.partial(prepare_kernel, slots, rows, cols, line),
        [((slots, terms), jnp.int32), requests],
        [pairing],
    )
    paired = is_power(cols) and cols > 1
    close = cols // 2 * slots if paired else cols * slots
    blank = cols * slots
    near_count = 3 * slots if line else slots
    far_count = 2 * CAP if line else rows * CAP
    right_count = near_count + far_count
    room = slots * terms + 4 * CHUNK
    plan, total = call(
        functools.partial(plan_kernel, near_count, close, blank),
        [((4 * room,), jnp.int32), ((4,), jnp.int32)],
        [table, term_count.reshape(1, slots)],
        smem=2,
        out_smem=True,
    )
    if line:
        outer = [(i, i ^ 1) for i in range(rows)]
        inner = [(1, 2), (2, 1)]
        partner = lax.ppermute(local, "row", outer)
        middle = lax.ppermute(local, "row", inner)
        asked = lax.ppermute(request, "row", outer)
        halved = call(relay_kernel, [blocks_of(slots // 2)] * 2, [total, partner], smem=1)
        passed = [lax.ppermute(piece, "row", inner) for piece in halved]
        (early,) = call(early_kernel, [blocks_of(CAP)], [asked, middle], smem=1)
        early = lax.ppermute(early, "row", outer)
        nears = [local, partner, middle]
        token = halved[0]
    else:
        asked = lax.all_to_all(request, "row", split_axis=0, concat_axis=0, tiled=True)
        picked = call(pick_far_kernel, [blocks_of(rows * CAP // 2)] * 2, [asked, local], smem=1)
        token = picked[0]
        nears = [local]
        fars = [
            [lax.all_to_all(piece, "row", split_axis=0, concat_axis=0, tiled=True)]
            for piece in picked
        ]
        far_panel = [fars[0][0], fars[1][0]]
    lefts = row_panel(local, cols, token)

    def panel(count):
        return pltpu.VMEM((count, extent, extent), local.dtype)

    near, left_panel, token = call(
        functools.partial(near_kernel, len(lefts)),
        [whole, blocks_of(blank + 1), ((8, LANES), jnp.float32)],
        [plan, total, *lefts, *nears],
        [panel(near_count)],
        smem=2,
    )
    sums, squares, crossed, lates = [], [], [], []
    for turn in range(2):
        if line:
            (late,) = call(late_kernel, [blocks_of(CAP // 2)], [asked, passed[turn], token], smem=1)
            token = late
            lates.append(lax.ppermute(late, "row", outer))
            far = [passed[turn], early, lates[turn]]
        else:
            far = fars[turn]
        total_half, stored = call(
            functools.partial(far_kernel, near_count, turn, line),
            [whole, blocks_of(slots // 2)],
            [plan, total, near, left_panel, (squares or [near])[-1], *far],
            [panel(right_count)],
            smem=2,
        )
        sums.append(total_half)
        squares.append(stored)
        if paired:
            crossed.append(cross(stored, cols))
    if line:
        far_panel = [*passed, early, *lates]
    if paired:
        closes = [spread(stored, cols // 2, cols) for stored in squares]
    else:
        closes = [row_panel(stored, cols) for stored in squares]
        crossed = squares
    if paired:
        crossed[0] = after(crossed[0], token, 0.3)
    partial_sum, right_panel, token = call(
        functools.partial(close_kernel, len(closes[0]), len(nears), line, blank),
        [whole, blocks_of(right_count), ((8, LANES), jnp.float32)],
        [plan, total, crossed[0], *sums, *closes[0], *closes[1], *nears, *far_panel],
        [panel(blank + 1)],
        smem=2,
        us=0,
    )
    distants = [[], []]
    if paired:
        crossed[1] = after(crossed[1], token)
        distants = [spread(piece, cols // 2, cols) for piece in crossed]
    (purified,) = call(
        functools.partial(distant_kernel, len(distants[0]), close),
        [((slots, extent, extent), local.dtype)],
        [plan, total, partial_sum, right_panel, *distants[0], *distants[1]],
        [panel(blank + 1 - close), pltpu.VMEM(*whole)],
        smem=2,
    )
    return purified.reshape(blocks.shape)


def spread(blocks, extent, cols):
    pieces = {0: blocks}
    bit = extent // 2
    while bit:
        for k in list(pieces):
            pieces[k ^ bit] = lax.ppermute(pieces[k], "col", [(i, i ^ bit) for i in range(cols)])
        bit //= 2
    return [pieces[k] for k in sorted(pieces)]


def solution(mesh):
    placed = (
        P(("sys", "row"), "col", None, None, None),
        P(("sys", "row"), "col", None, None, None),
        P(("sys", "row"), "col", None),
    )
    return jax.shard_map(
        per_device,
        mesh=mesh,
        in_specs=placed,
        out_specs=P(("sys", "row"), "col", None, None, None),
        check_vma=False,
    )
```

time: 151 us -> 56.9 us (0.38)
  waiting for transfers between devices: 48.9 us -> 11.8 us
  local copies, waits for them, and re-layouts: 34.6 us -> 0.87 us
  other arithmetic: 26 us -> 0 us
  Pallas kernels: 0 us -> 21.6 us
  matrix products: 17.9 us -> 0 us
  between operations: 13.5 us -> 0.16 us
  starting transfers between devices: 9.9 us -> 22.2 us
    gather x5 -> x0, local copies, waits for them, and re-layouts: 32.8 us -> none  [the longest x2 20.6 us: stacked_product(): jnp.take(left_panel, left_index.reshape(-1), axis=0)]
    all_to_all x2 -> x0, waiting for transfers between devices: 26.3 us -> none  [the longest x1 21.5 us: per_device(): lax.all_to_all(reply, 'row', split_axis=0, concat_axis=0, tiled=True)]
    select_n x8 -> x0, other arithmetic: 23.5 us -> none  [the longest x3 14.9 us: stacked_product(): jnp.take(left_panel, left_index.reshape(-1), axis=0)]
    ppermute x0 -> x17, starting transfers between devices: none -> 22.2 us  [the longest x2 6.42 us: per_device(): lates.append(lax.ppermute(late, 'row', outer))]
    all_gather x2 -> x0, waiting for transfers between devices: 21.9 us -> none  [the longest x1 21.9 us: per_device(): lax.all_gather(square_stored, 'col', axis=1, tiled=True)]
    pallas_call x0 -> x14, Pallas kernels: none -> 21.6 us  [the longest x11 21.6 us: call(): pl.pallas_call(kernel, out_shape=[jax.ShapeDtypeStruct(shape, dtype) for...]
    dot_general x2 -> x0, matrix products: 17.9 us -> none  [stacked_product(): jnp.einsum('stij,stjk->sik', left_stack, right_stack, preferred_element_t...]
    ppermute x0 -> x17, waiting for transfers between devices: none -> 11.8 us  [the longest x3 5.35 us: cross(): lax.ppermute(blocks, 'col', [(i, i ^ cols // 2) for i in range(cols)])]
  transfers between devices with their start and end apart: 4 -> 17, of which waited for: 3 -> 7; matrix products, arithmetic and copies ran while one was open for 15% -> 0% of each run, Pallas kernels for 0% -> 33%
where the time goes in v2:
time: 56.9 us; the launch traced here: 56.6 us
  starting transfers between devices  22.2 us (39%)
  Pallas kernels  21.6 us (38%)
  waiting for transfers between devices  11.8 us (21%)
  local copies, waits for them, and re-layouts  0.87 us (2%)
    pallas_call x11, Pallas kernels, call(): pl.pallas_call(kernel, out_shape=[jax.ShapeDtypeStruct(shape, dtype) for...  21.6 us
    ppermute x2, starting transfers between devices, per_device(): lates.append(lax.ppermute(late, 'row', outer))  6.42 us
    ppermute x3, waiting for transfers between devices, cross(): lax.ppermute(blocks, 'col', [(i, i ^ cols // 2) for i in range(cols)])  5.35 us
    ppermute x1, starting transfers between devices, per_device(): early = lax.ppermute(early, 'row', outer)  4.58 us
    ppermute x3, starting transfers between devices, cross(): lax.ppermute(blocks, 'col', [(i, i ^ cols // 2) for i in range(cols)])  3.64 us
    ppermute x1, waiting for transfers between devices, per_device(): partner = lax.ppermute(local, 'row', outer)  3.31 us
    ppermute x1, starting transfers between devices, per_device(): partner = lax.ppermute(local, 'row', outer)  3.02 us
    ppermute x1, waiting for transfers between devices, per_device(): asked = lax.ppermute(request, 'row', outer)  1.7 us
  transfers between devices with their start and end apart: 17, of which 7 were waited for; matrix products, arithmetic and copies ran while one was open for 0% of the time, Pallas kernels for 33%

profile of v2, /device:TPU:0, one launch (start us, length us, event | category | flops | bytes accessed | tf_op | source)
XLA Modules:
  0.0 56.6 jit_solution(1070481949313024506)
XLA Ops:
  0.0 3.0 %collective-permute-start.2 = (bf16[16,128,128]{2,1,0:T(8,128)(2,1)}, bf16[16,128,128]{2,1,0:T(8,128)(2,1)S(1)}, u32[]{:S(2)}, u32[]{:S(2)}) collective-permute-start(bf16[16,128,128]{2,1,0:T(8,128)(2,1)} %bitcast.6), channel_id=1, source_target_pairs={{0,4},{4,0},{8,12},{12,8},{1,5},{5,1},{9,13},{13,9},{2,6},{6,2},{1... | collective-permute-start | bytes 1572872 | tf_op jit(solution)/shard_map/ppermute | solution.py:378
  3.0 1.5 %collective-permute-start.1 = (bf16[16,128,128]{2,1,0:T(8,128)(2,1)}, bf16[16,128,128]{2,1,0:T(8,128)(2,1)S(1)}, u32[]{:S(2)}, u32[]{:S(2)}) collective-permute-start(bf16[16,128,128]{2,1,0:T(8,128)(2,1)} %bitcast.7), channel_id=1, source_target_pairs={{0,2},{1,3},{2,0},{3,1},{4,6},{5,7},{6,4},{7,5},{8,10},{9,11},{10,... | collective-permute-start | bytes 1572872 | tf_op jit(solution)/shard_map/ppermute | solution.py:326
  4.5 0.7 %collective-permute-start.4 = (bf16[16,128,128]{2,1,0:T(8,128)(2,1)}, bf16[16,128,128]{2,1,0:T(8,128)(2,1)S(1)}, u32[]{:S(2)}, u32[]{:S(2)}) collective-permute-start(bf16[16,128,128]{2,1,0:T(8,128)(2,1)} %bitcast.8), channel_id=1, source_target_pairs={{4,8},{8,4},{5,9},{9,5},{6,10},{10,6},{7,11},{11,7},{20,24},{24,20... | collective-permute-start | bytes 1572872 | tf_op jit(solution)/shard_map/ppermute | solution.py:379
  5.3 0.7 %copy-done.1 = s32[1,1,16,16,2]{3,4,2,1,0:T(2,128)S(1)} copy-done((s32[1,1,16,16,2]{3,4,2,1,0:T(2,128)S(1)}, s32[1,1,16,16,2]{3,4,2,1,0:T(2,128)}, u32[]{:S(2)}) %copy-start.1) | copy-done | bytes 2072
  6.0 0.5 shard_map.37
  6.7 5.2 %shard_map.38 = (s32[1280]{0:T(1024)S(1)}, s32[4]{0:T(128)S(1)}) custom-call(s32[16,16]{1,0:T(8,128)S(1)} %get-tuple-element.21.table_ref, s32[1,16]{1,0:T(1,128)S(1)} %bitcast.14), custom_call_target="tpu_custom_call" | custom-call | flops 2000099968 | bytes 6001000 | tf_op jit(solution)/shard_map/pallas_call | solution.py:341
  11.8 3.3 %collective-permute-done.2.partner_ref.refs_5_.refs_7_ = bf16[16,128,128]{2,1,0:T(8,128)(2,1)S(1)} collective-permute-done((bf16[16,128,128]{2,1,0:T(8,128)(2,1)}, bf16[16,128,128]{2,1,0:T(8,128)(2,1)S(1)}, u32[]{:S(2)}, u32[]{:S(2)}) %collective-permute-start.2) | collective-permute-done | bytes 524320 | tf_op jit(solution)/shard_map/ppermute | solution.py:378
  15.2 0.6 shard_map.39
  15.7 0.9 %collective-permute-done.1.value_ref = bf16[16,128,128]{2,1,0:T(8,128)(2,1)S(1)} collective-permute-done((bf16[16,128,128]{2,1,0:T(8,128)(2,1)}, bf16[16,128,128]{2,1,0:T(8,128)(2,1)S(1)}, u32[]{:S(2)}, u32[]{:S(2)}) %collective-permute-start.1) | collective-permute-done | bytes 524320 | tf_op jit(solution)/shard_map/ppermute | solution.py:326
  16.6 1.2 %collective-permute-start.6 = (s32[2,128]{1,0:T(2,128)S(1)}, s32[2,128]{1,0:T(2,128)S(1)}, u32[]{:S(2)}, u32[]{:S(2)}) collective-permute-start(s32[2,128]{1,0:T(2,128)S(1)} %get-tuple-element.27), channel_id=1, source_target_pairs={{0,4},{4,0},{8,12},{12,8},{1,5},{5,1},{9,13},{13,9},{2,6},{6,2},{1... | collective-permute-start | bytes 3080 | tf_op jit(solution)/shard_map/ppermute | solution.py:380
  17.8 0.7 %collective-permute-start.5 = (bf16[8,128,128]{2,1,0:T(8,128)(2,1)S(1)}, bf16[8,128,128]{2,1,0:T(8,128)(2,1)S(1)}, u32[]{:S(2)}, u32[]{:S(2)}) collective-permute-start(bf16[8,128,128]{2,1,0:T(8,128)(2,1)S(1)} %get-tuple-element.24.after_ref), channel_id=1, source_target_pairs={{4,8},{8,4},{5,9},{9,5},{6,10},{10,6},{7,11},{11,7},{20,24},{24,20... | collective-permute-start | bytes 786440 | tf_op jit(solution)/shard_map/ppermute | solution.py:382
  18.5 1.7 %collective-permute-done.6.asked_ref = s32[2,128]{1,0:T(2,128)S(1)} collective-permute-done((s32[2,128]{1,0:T(2,128)S(1)}, s32[2,128]{1,0:T(2,128)S(1)}, u32[]{:S(2)}, u32[]{:S(2)}) %collective-permute-start.6) | collective-permute-done | bytes 1056 | tf_op jit(solution)/shard_map/ppermute | solution.py:380
  20.2 0.8 %collective-permute-start.10 = (bf16[8,128,128]{2,1,0:T(8,128)(2,1)S(1)}, bf16[8,128,128]{2,1,0:T(8,128)(2,1)S(1)}, u32[]{:S(2)}, u32[]{:S(2)}) collective-permute-start(bf16[8,128,128]{2,1,0:T(8,128)(2,1)S(1)} %get-tuple-element.30), channel_id=1, source_target_pairs={{4,8},{8,4},{5,9},{9,5},{6,10},{10,6},{7,11},{11,7},{20,24},{24,20... | collective-permute-start | bytes 786440 | tf_op jit(solution)/shard_map/ppermute | solution.py:382
  21.0 0.6 shard_map.42
  21.6 4.6 %collective-permute-start.7 = (bf16[8,128,128]{2,1,0:T(8,128)(2,1)S(1)}, bf16[8,128,128]{2,1,0:T(8,128)(2,1)S(1)}, u32[]{:S(2)}, u32[]{:S(2)}) collective-permute-start(bf16[8,128,128]{2,1,0:T(8,128)(2,1)S(1)} %shard_map.42), channel_id=1, source_target_pairs={{0,4},{4,0},{8,12},{12,8},{1,5},{5,1},{9,13},{13,9},{2,6},{6,2},{1... | collective-permute-start | bytes 786440 | tf_op jit(solution)/shard_map/ppermute | solution.py:384
  26.2 2.0 %shard_map.41 = (f32[16,128,128]{2,1,0:T(8,128)S(1)}, bf16[65,128,128]{2,1,0:T(8,128)(2,1)S(1)}, f32[8,128]{1,0:T(8,128)S(1)}) custom-call(s32[1280]{0:T(1024)S(1)} %get-tuple-element.22.plan_ref, s32[4]{0:T(128)S(1)} %get-tuple-element.23.after_ref.total_ref, bf16[16,128,128]{2,1,0:T(8,128)(2,1)S(1)} %bitcast.10, ...), custom_call_target="tpu_custom_call" | custom-call | flops 2000099968 | bytes 6001000 | tf_op jit(solution)/shard_map/pallas_call | solution.py:341
  28.2 0.6 shard_map.43.after_ref
  28.8 1.8 %collective-permute-start.8 = (bf16[4,128,128]{2,1,0:T(8,128)(2,1)S(1)}, bf16[4,128,128]{2,1,0:T(8,128)(2,1)S(1)}, u32[]{:S(2)}, u32[]{:S(2)}) collective-permute-start(bf16[4,128,128]{2,1,0:T(8,128)(2,1)S(1)} %shard_map.43.after_ref), channel_id=1, source_target_pairs={{0,4},{4,0},{8,12},{12,8},{1,5},{5,1},{9,13},{13,9},{2,6},{6,2},{1... | collective-permute-start | bytes 393224 | tf_op jit(solution)/shard_map/ppermute | solution.py:414
  30.6 0.6 shard_map.45.after_ref
  31.2 4.6 %collective-permute-start.11 = (bf16[4,128,128]{2,1,0:T(8,128)(2,1)S(1)}, bf16[4,128,128]{2,1,0:T(8,128)(2,1)S(1)}, u32[]{:S(2)}, u32[]{:S(2)}) collective-permute-start(bf16[4,128,128]{2,1,0:T(8,128)(2,1)S(1)} %shard_map.45.after_ref), channel_id=1, source_target_pairs={{0,4},{4,0},{8,12},{12,8},{1,5},{5,1},{9,13},{13,9},{2,6},{6,2},{1... | collective-permute-start | bytes 393224 | tf_op jit(solution)/shard_map/ppermute | solution.py:414
  35.8 2.6 %shard_map.44 = (f32[16,128,128]{2,1,0:T(8,128)S(1)}, bf16[8,128,128]{2,1,0:T(8,128)(2,1)S(1)}) custom-call(s32[1280]{0:T(1024)S(1)} %get-tuple-element.22.plan_ref, s32[4]{0:T(128)S(1)} %get-tuple-element.23.after_ref.total_ref, f32[16,128,128]{2,1,0:T(8,128)S(1)} %get-tuple-element.25.near_ref.after_ref, ...), custom_call_target="tpu_custom_call" | custom-call | flops 2000099968 | bytes 6001000 | tf_op jit(solution)/shard_map/pallas_call | solution.py:341
  38.4 1.6 %collective-permute-start.9 = (bf16[8,128,128]{2,1,0:T(8,128)(2,1)S(1)}, bf16[8,128,128]{2,1,0:T(8,128)(2,1)S(1)}, u32[]{:S(2)}, u32[]{:S(2)}) collective-permute-start(bf16[8,128,128]{2,1,0:T(8,128)(2,1)S(1)} %get-tuple-element.29.after_ref.refs_2_), channel_id=1, source_target_pairs={{0,2},{1,3},{2,0},{3,1},{4,6},{5,7},{6,4},{7,5},{8,10},{9,11},{10,... | collective-permute-start | bytes 786440 | tf_op jit(solution)/shard_map/ppermute | solution.py:326
  40.0 2.9 %shard_map.47 = (f32[16,128,128]{2,1,0:T(8,128)S(1)}, bf16[8,128,128]{2,1,0:T(8,128)(2,1)S(1)}) custom-call(s32[1280]{0:T(1024)S(1)} %get-tuple-element.22.plan_ref, s32[4]{0:T(128)S(1)} %get-tuple-element.23.after_ref.total_ref, f32[16,128,128]{2,1,0:T(8,128)S(1)} %get-tuple-element.25.near_ref.after_ref, ...), custom_call_target="tpu_custom_call" | custom-call | flops 2000099968 | bytes 6001000 | tf_op jit(solution)/shard_map/pallas_call | solution.py:341
  43.0 0.5 collective-permute-start.12
  43.5 0.6 %collective-permute-start.15 = (bf16[8,128,128]{2,1,0:T(8,128)(2,1)S(1)}, bf16[8,128,128]{2,1,0:T(8,128)(2,1)S(1)}, u32[]{:S(2)}, u32[]{:S(2)}) collective-permute-start(bf16[8,128,128]{2,1,0:T(8,128)(2,1)S(1)} %get-tuple-element.33.refs_4_), channel_id=1, source_target_pairs={{0,2},{1,3},{2,0},{3,1},{4,6},{5,7},{6,4},{7,5},{8,10},{9,11},{10,... | collective-permute-start | bytes 786440 | tf_op jit(solution)/shard_map/ppermute | solution.py:326
  44.1 1.8 %collective-permute-done.9.value_ref = bf16[8,128,128]{2,1,0:T(8,128)(2,1)S(1)} collective-permute-done((bf16[8,128,128]{2,1,0:T(8,128)(2,1)S(1)}, bf16[8,128,128]{2,1,0:T(8,128)(2,1)S(1)}, u32[]{:S(2)}, u32[]{:S(2)}) %collective-permute-start.9) | collective-permute-done | bytes 262176 | tf_op jit(solution)/shard_map/ppermute | solution.py:326
  45.8 3.2 %shard_map.48 = (f32[16,128,128]{2,1,0:T(8,128)S(1)}, bf16[64,128,128]{2,1,0:T(8,128)(2,1)S(1)}, f32[8,128]{1,0:T(8,128)S(1)}) custom-call(s32[1280]{0:T(1024)S(1)} %get-tuple-element.22.plan_ref, s32[4]{0:T(128)S(1)} %get-tuple-element.23.after_ref.total_ref, bf16[8,128,128]{2,1,0:T(8,128)(2,1)S(1)} %shard_map.46.after_ref.refs_0_, ...), custom_call_target="tpu_custom_call" | custom-call | flops 100000 | bytes 1000 | tf_op jit(solution)/shard_map/pallas_call | solution.py:341
  49.1 2.7 %collective-permute-done.15.value_ref = bf16[8,128,128]{2,1,0:T(8,128)(2,1)S(1)} collective-permute-done((bf16[8,128,128]{2,1,0:T(8,128)(2,1)S(1)}, bf16[8,128,128]{2,1,0:T(8,128)(2,1)S(1)}, u32[]{:S(2)}, u32[]{:S(2)}) %collective-permute-start.15) | collective-permute-done | bytes 262176 | tf_op jit(solution)/shard_map/ppermute | solution.py:326
  51.8 0.5 collective-permute-start.14
  52.3 1.0 %collective-permute-done.16.refs_3_ = bf16[8,128,128]{2,1,0:T(8,128)(2,1)S(1)} collective-permute-done((bf16[8,128,128]{2,1,0:T(8,128)(2,1)S(1)}, bf16[8,128,128]{2,1,0:T(8,128)(2,1)S(1)}, u32[]{:S(2)}, u32[]{:S(2)}) %collective-permute-start.16) | collective-permute-done | bytes 262176 | tf_op jit(solution)/shard_map/ppermute | solution.py:465
  53.3 0.4 collective-permute-done.14.refs_1_
  53.7 2.9 %shard_map.50 = bf16[16,128,128]{2,1,0:T(8,128)(2,1)} custom-call(s32[1280]{0:T(1024)S(1)} %get-tuple-element.22.plan_ref, s32[4]{0:T(128)S(1)} %get-tuple-element.23.after_ref.total_ref, f32[16,128,128]{2,1,0:T(8,128)S(1)} %get-tuple-element.34.close_ref, bf16[64,128,128]{2,1,0:T(8,128)(2,1)S(1)} %get-tuple-element.35.right_ref, ...), custom_call_target="tpu_custom_call" | custom-call | flops 2000099968 | bytes 6001000 | tf_op jit(solution)/shard_map/pallas_call | solution.py:341
  (22 shorter events, 0.3 us)
Async XLA Ops:
  0.0 15.2 %collective-permute-start.2 = (bf16[16,128,128]{2,1,0:T(8,128)(2,1)}, bf16[16,128,128]{2,1,0:T(8,128)(2,1)S(1)}, u32[]{:S(2)}, u32[]{:S(2)}) collective-permute-start(bf16[16,128,128]{2,1,0:T(8,128)(2,1)} %bitcast.6), channel_id=1, source_target_pairs={{0,4},{4,0},{8,12},{12,8},{1,5},{5,1},{9,13},{13,9},{2,6},{6,2},{1... | collective-permute-start | bytes 1572872 | tf_op jit(solution)/shard_map/ppermute | solution.py:378
  3.0 13.6 %collective-permute-start.1 = (bf16[16,128,128]{2,1,0:T(8,128)(2,1)}, bf16[16,128,128]{2,1,0:T(8,128)(2,1)S(1)}, u32[]{:S(2)}, u32[]{:S(2)}) collective-permute-start(bf16[16,128,128]{2,1,0:T(8,128)(2,1)} %bitcast.7), channel_id=1, source_target_pairs={{0,2},{1,3},{2,0},{3,1},{4,6},{5,7},{6,4},{7,5},{8,10},{9,11},{10,... | collective-permute-start | bytes 1572872 | tf_op jit(solution)/shard_map/ppermute | solution.py:326
  4.5 16.5 %collective-permute-start.4 = (bf16[16,128,128]{2,1,0:T(8,128)(2,1)}, bf16[16,128,128]{2,1,0:T(8,128)(2,1)S(1)}, u32[]{:S(2)}, u32[]{:S(2)}) collective-permute-start(bf16[16,128,128]{2,1,0:T(8,128)(2,1)} %bitcast.8), channel_id=1, source_target_pairs={{4,8},{8,4},{5,9},{9,5},{6,10},{10,6},{7,11},{11,7},{20,24},{24,20... | collective-permute-start | bytes 1572872 | tf_op jit(solution)/shard_map/ppermute | solution.py:379
  5.2 21.0 %collective-permute-start = (bf16[16,128,128]{2,1,0:T(8,128)(2,1)}, bf16[16,128,128]{2,1,0:T(8,128)(2,1)S(1)}, u32[]{:S(2)}, u32[]{:S(2)}) collective-permute-start(bf16[16,128,128]{2,1,0:T(8,128)(2,1)} %bitcast.9), channel_id=1, source_target_pairs={{0,1},{1,0},{2,3},{3,2},{4,5},{5,4},{6,7},{7,6},{8,9},{9,8},{10,11... | collective-permute-start | bytes 1572872 | tf_op jit(solution)/shard_map/ppermute | solution.py:465
  5.3 0.7 %copy-start.1 = (s32[1,1,16,16,2]{3,4,2,1,0:T(2,128)S(1)}, s32[1,1,16,16,2]{3,4,2,1,0:T(2,128)}, u32[]{:S(2)}) copy-start(s32[1,1,16,16,2]{3,4,2,1,0:T(2,128)} %param.4) | copy-start | bytes 6148
  6.0 0.7 %copy-start.2 = (s32[1,1,16]{2,1,0:T(1,128)S(1)}, s32[1,1,16]{2,1,0:T(1,128)}, u32[]{:S(2)}) copy-start(s32[1,1,16]{2,1,0:T(1,128)} %param.5) | copy-start | bytes 196
  16.6 9.5 %collective-permute-start.3 = (bf16[16,128,128]{2,1,0:T(8,128)(2,1)S(1)}, bf16[16,128,128]{2,1,0:T(8,128)(2,1)S(1)}, u32[]{:S(2)}, u32[]{:S(2)}) collective-permute-start(bf16[16,128,128]{2,1,0:T(8,128)(2,1)S(1)} %shard_map.40.refs_2_), channel_id=1, source_target_pairs={{0,1},{1,0},{2,3},{3,2},{4,5},{5,4},{6,7},{7,6},{8,9},{9,8},{10,11... | collective-permute-start | bytes 1572872 | tf_op jit(solution)/shard_map/ppermute | solution.py:465
  16.6 3.6 %collective-permute-start.6 = (s32[2,128]{1,0:T(2,128)S(1)}, s32[2,128]{1,0:T(2,128)S(1)}, u32[]{:S(2)}, u32[]{:S(2)}) collective-permute-start(s32[2,128]{1,0:T(2,128)S(1)} %get-tuple-element.27), channel_id=1, source_target_pairs={{0,4},{4,0},{8,12},{12,8},{1,5},{5,1},{9,13},{13,9},{2,6},{6,2},{1... | collective-permute-start | bytes 3080 | tf_op jit(solution)/shard_map/ppermute | solution.py:380
  17.8 10.4 %collective-permute-start.5 = (bf16[8,128,128]{2,1,0:T(8,128)(2,1)S(1)}, bf16[8,128,128]{2,1,0:T(8,128)(2,1)S(1)}, u32[]{:S(2)}, u32[]{:S(2)}) collective-permute-start(bf16[8,128,128]{2,1,0:T(8,128)(2,1)S(1)} %get-tuple-element.24.after_ref), channel_id=1, source_target_pairs={{4,8},{8,4},{5,9},{9,5},{6,10},{10,6},{7,11},{11,7},{20,24},{24,20... | collective-permute-start | bytes 786440 | tf_op jit(solution)/shard_map/ppermute | solution.py:382
  20.2 6.0 %copy-start = (bf16[1,1,16,128,128]{4,3,2,1,0:T(8,128)(2,1)S(1)}, bf16[1,1,16,128,128]{4,3,2,1,0:T(8,128)(2,1)}, u32[]{:S(2)}) copy-start(bf16[1,1,16,128,128]{4,3,2,1,0:T(8,128)(2,1)} %param.3) | copy-start | bytes 1572868
  20.2 10.4 %collective-permute-start.10 = (bf16[8,128,128]{2,1,0:T(8,128)(2,1)S(1)}, bf16[8,128,128]{2,1,0:T(8,128)(2,1)S(1)}, u32[]{:S(2)}, u32[]{:S(2)}) collective-permute-start(bf16[8,128,128]{2,1,0:T(8,128)(2,1)S(1)} %get-tuple-element.30), channel_id=1, source_target_pairs={{4,8},{8,4},{5,9},{9,5},{6,10},{10,6},{7,11},{11,7},{20,24},{24,20... | collective-permute-start | bytes 786440 | tf_op jit(solution)/shard_map/ppermute | solution.py:382
  21.6 14.2 %collective-permute-start.7 = (bf16[8,128,128]{2,1,0:T(8,128)(2,1)S(1)}, bf16[8,128,128]{2,1,0:T(8,128)(2,1)S(1)}, u32[]{:S(2)}, u32[]{:S(2)}) collective-permute-start(bf16[8,128,128]{2,1,0:T(8,128)(2,1)S(1)} %shard_map.42), channel_id=1, source_target_pairs={{0,4},{4,0},{8,12},{12,8},{1,5},{5,1},{9,13},{13,9},{2,6},{6,2},{1... | collective-permute-start | bytes 786440 | tf_op jit(solution)/shard_map/ppermute | solution.py:384
  28.8 7.0 %collective-permute-start.8 = (bf16[4,128,128]{2,1,0:T(8,128)(2,1)S(1)}, bf16[4,128,128]{2,1,0:T(8,128)(2,1)S(1)}, u32[]{:S(2)}, u32[]{:S(2)}) collective-permute-start(bf16[4,128,128]{2,1,0:T(8,128)(2,1)S(1)} %shard_map.43.after_ref), channel_id=1, source_target_pairs={{0,4},{4,0},{8,12},{12,8},{1,5},{5,1},{9,13},{13,9},{2,6},{6,2},{1... | collective-permute-start | bytes 393224 | tf_op jit(solution)/shard_map/ppermute | solution.py:414
  31.2 8.8 %collective-permute-start.11 = (bf16[4,128,128]{2,1,0:T(8,128)(2,1)S(1)}, bf16[4,128,128]{2,1,0:T(8,128)(2,1)S(1)}, u32[]{:S(2)}, u32[]{:S(2)}) collective-permute-start(bf16[4,128,128]{2,1,0:T(8,128)(2,1)S(1)} %shard_map.45.after_ref), channel_id=1, source_target_pairs={{0,4},{4,0},{8,12},{12,8},{1,5},{5,1},{9,13},{13,9},{2,6},{6,2},{1... | collective-permute-start | bytes 393224 | tf_op jit(solution)/shard_map/ppermute | solution.py:414
  38.4 7.4 %collective-permute-start.9 = (bf16[8,128,128]{2,1,0:T(8,128)(2,1)S(1)}, bf16[8,128,128]{2,1,0:T(8,128)(2,1)S(1)}, u32[]{:S(2)}, u32[]{:S(2)}) collective-permute-start(bf16[8,128,128]{2,1,0:T(8,128)(2,1)S(1)} %get-tuple-element.29.after_ref.refs_2_), channel_id=1, source_target_pairs={{0,2},{1,3},{2,0},{3,1},{4,6},{5,7},{6,4},{7,5},{8,10},{9,11},{10,... | collective-permute-start | bytes 786440 | tf_op jit(solution)/shard_map/ppermute | solution.py:326
  42.9 3.0 %collective-permute-start.13 = (bf16[8,128,128]{2,1,0:T(8,128)(2,1)S(1)}, bf16[8,128,128]{2,1,0:T(8,128)(2,1)S(1)}, u32[]{:S(2)}, u32[]{:S(2)}) collective-permute-start(bf16[8,128,128]{2,1,0:T(8,128)(2,1)S(1)} %get-tuple-element.33.refs_4_), channel_id=1, source_target_pairs={{0,1},{1,0},{2,3},{3,2},{4,5},{5,4},{6,7},{7,6},{8,9},{9,8},{10,11... | collective-permute-start | bytes 786440 | tf_op jit(solution)/shard_map/ppermute | solution.py:465
  43.0 2.9 %collective-permute-start.12 = (bf16[8,128,128]{2,1,0:T(8,128)(2,1)S(1)}, bf16[8,128,128]{2,1,0:T(8,128)(2,1)S(1)}, u32[]{:S(2)}, u32[]{:S(2)}) collective-permute-start(bf16[8,128,128]{2,1,0:T(8,128)(2,1)S(1)} %get-tuple-element.29.after_ref.refs_2_), channel_id=1, source_target_pairs={{0,1},{1,0},{2,3},{3,2},{4,5},{5,4},{6,7},{7,6},{8,9},{9,8},{10,11... | collective-permute-start | bytes 786440 | tf_op jit(solution)/shard_map/ppermute | solution.py:465
  43.5 8.3 %collective-permute-start.15 = (bf16[8,128,128]{2,1,0:T(8,128)(2,1)S(1)}, bf16[8,128,128]{2,1,0:T(8,128)(2,1)S(1)}, u32[]{:S(2)}, u32[]{:S(2)}) collective-permute-start(bf16[8,128,128]{2,1,0:T(8,128)(2,1)S(1)} %get-tuple-element.33.refs_4_), channel_id=1, source_target_pairs={{0,2},{1,3},{2,0},{3,1},{4,6},{5,7},{6,4},{7,5},{8,10},{9,11},{10,... | collective-permute-start | bytes 786440 | tf_op jit(solution)/shard_map/ppermute | solution.py:326
  51.8 1.5 %collective-permute-start.16 = (bf16[8,128,128]{2,1,0:T(8,128)(2,1)S(1)}, bf16[8,128,128]{2,1,0:T(8,128)(2,1)S(1)}, u32[]{:S(2)}, u32[]{:S(2)}) collective-permute-start(bf16[8,128,128]{2,1,0:T(8,128)(2,1)S(1)} %shard_map.49.refs_2_), channel_id=1, source_target_pairs={{0,1},{1,0},{2,3},{3,2},{4,5},{5,4},{6,7},{7,6},{8,9},{9,8},{10,11... | collective-permute-start | bytes 786440 | tf_op jit(solution)/shard_map/ppermute | solution.py:465
  51.8 1.9 %collective-permute-start.14 = (bf16[8,128,128]{2,1,0:T(8,128)(2,1)S(1)}, bf16[8,128,128]{2,1,0:T(8,128)(2,1)S(1)}, u32[]{:S(2)}, u32[]{:S(2)}) collective-permute-start(bf16[8,128,128]{2,1,0:T(8,128)(2,1)S(1)} %shard_map.46.after_ref.refs_0_), channel_id=1, source_target_pairs={{0,1},{1,0},{2,3},{3,2},{4,5},{5,4},{6,7},{7,6},{8,9},{9,8},{10,11... | collective-permute-start | bytes 786440 | tf_op jit(solution)/shard_map/ppermute | solution.py:465

commit v3 on v2

--- a/solution.py
+++ b/solution.py
@@ -15,6 +15,7 @@
 FIELD = 1024
 SMEM = pl.BlockSpec(memory_space=pltpu.SMEM)
 VMEM = pl.BlockSpec(memory_space=pltpu.VMEM)
+ANY = pl.BlockSpec(memory_space=pl.ANY)
 
 
 def params(limit):
@@ -76,9 +77,10 @@
         table_ref[s : s + 1, :] = left + FIELD * (right + FIELD * s)
 
 
-def plan_kernel(near, close, blank, table_ref, count_ref, plan_ref, total_ref):
+def plan_kernel(near, close, blank, table_ref, count_ref, plan_ref, token_ref):
     slots = table_ref.shape[0]
-    room = plan_ref.shape[0] // 4
+    room = plan_ref.shape[0] // 4 - LANES // 4
+    token_ref[0] = 0
 
     def blank_of(s):
         return blank + FIELD * FIELD * s
@@ -100,7 +102,7 @@
 
     ends = lax.fori_loop(0, slots, block, tuple(jnp.int32(i * room) for i in range(4)))
     for i, end in enumerate(ends):
-        total_ref[i] = end - i * room
+        plan_ref[4 * room + i] = end - i * room
 
         def pad(j, carry, end=end):
             plan_ref[end + j] = blank
@@ -160,6 +162,17 @@
     def _():
         for p in range(CAP // 2):
             out_ref[p] = jnp.concatenate([side(2 * p), side(2 * p + 1)], axis=1)
+
+
+def choose_kernel(ends_ref, middles_ref, after_ref, *out_refs):
+    row = lax.axis_index("row")
+    for is_end, piece_ref in ((True, ends_ref), (False, middles_ref)):
+
+        @pl.when(((row == 0) | (row == 3)) == is_end)
+        def _():
+            for i, out_ref in enumerate(out_refs):
+                count = out_ref.shape[0]
+                out_ref[...] = piece_ref[i * count : (i + 1) * count]
 
 
 def fill(panel_ref, piece_refs):
@@ -176,15 +189,25 @@
     return jnp.concatenate([block[:, half:], block[:, :half]], axis=1)
 
 
-def add_products(plan_ref, total_ref, which, left_ref, right_ref, sum_ref, left_shift=0):
-    room = plan_ref.shape[0] // 4
+def fetch(plan_ref, lists_ref, semaphore):
+    copy = pltpu.make_async_copy(plan_ref, lists_ref, semaphore)
+    copy.start()
+    return copy
+
+
+def room_of(lists_ref):
+    return lists_ref.shape[0] // 4 - LANES // 4
+
+
+def add_products(lists_ref, which, left_ref, right_ref, sum_ref, start=0):
+    room = room_of(lists_ref)
 
     def step(c, carry):
         for p in range(CHUNK):
-            first = plan_ref[which * room + 2 * (c * CHUNK + p)]
-            second = plan_ref[which * room + 2 * (c * CHUNK + p) + 1]
+            first = lists_ref[which * room + 2 * (c * CHUNK + p)]
+            second = lists_ref[which * room + 2 * (c * CHUNK + p) + 1]
             left = jnp.concatenate(
-                [left_ref[word % FIELD - left_shift] for word in (first, second)], axis=1
+                [left_ref[word % FIELD - start] for word in (first, second)], axis=1
             )
             right = jnp.concatenate(
                 [right_ref[(word // FIELD) % FIELD] for word in (first, second)], axis=0
@@ -194,18 +217,21 @@
             )
         return carry
 
-    lax.fori_loop(0, (total_ref[which] + 2 * CHUNK - 1) // (2 * CHUNK), step, 0)
-
-
-def near_kernel(lefts, plan_ref, total_ref, *refs):
-    left_refs, right_refs = refs[:lefts], refs[lefts:-4]
-    sum_ref, left_ref, token_ref, right_ref = refs[-4:]
+    count = lists_ref[4 * room + which]
+    lax.fori_loop(0, (count + 2 * CHUNK - 1) // (2 * CHUNK), step, 0)
+
+
+def near_kernel(lefts, plan_ref, *refs):
+    left_refs, right_refs = refs[:lefts], refs[lefts:-6]
+    sum_ref, left_ref, token_ref, right_ref, lists_ref, semaphore = refs[-6:]
+    copy = fetch(plan_ref, lists_ref, semaphore)
     token_ref[...] = jnp.zeros(token_ref.shape, token_ref.dtype)
     at = fill(left_ref, left_refs)
     left_ref[at] = jnp.zeros(left_ref.shape[1:], left_ref.dtype)
     fill(right_ref, right_refs)
     sum_ref[...] = jnp.zeros(sum_ref.shape, sum_ref.dtype)
-    add_products(plan_ref, total_ref, 0, left_ref, right_ref, sum_ref)
+    copy.wait()
+    add_products(lists_ref, 0, left_ref, right_ref, sum_ref)
 
 
 def unpack(panel_ref, at, piece_ref, first, count):
@@ -215,9 +241,10 @@
         panel_ref[at + 2 * p + 1] = turned(both)
 
 
-def far_kernel(start, turn, line, plan_ref, total_ref, near_ref, left_ref, after_ref, *refs):
-    far_refs = refs[:-3]
-    sum_ref, stored_ref, right_ref = refs[-3:]
+def far_kernel(start, turn, line, plan_ref, near_ref, left_ref, after_ref, *refs):
+    far_refs = refs[:-5]
+    sum_ref, stored_ref, right_ref, lists_ref, semaphore = refs[-5:]
+    copy = fetch(plan_ref, lists_ref, semaphore)
     right_ref[0] = jnp.zeros(right_ref.shape[1:], right_ref.dtype)
     if line:
         row = lax.axis_index("row")
@@ -234,7 +261,8 @@
         unpack(right_ref, start, far_refs[0], 0, far_refs[0].shape[0])
     for s in range(sum_ref.shape[0]):
         sum_ref[s] = turned(near_ref[s]) if turn else near_ref[s]
-    add_products(plan_ref, total_ref, 1, left_ref, right_ref, sum_ref)
+    copy.wait()
+    add_products(lists_ref, 1, left_ref, right_ref, sum_ref)
     half = sum_ref.shape[-1] // 2
     for p in range(stored_ref.shape[0]):
         both = [sum_ref[2 * p][:, :half], sum_ref[2 * p + 1][:, :half]]
@@ -248,8 +276,9 @@
         )
 
 
-def close_kernel(closes, nears, line, blank, plan_ref, total_ref, after_ref, *refs):
-    refs, (sum_ref, right_ref, token_ref, left_ref) = refs[:-4], refs[-4:]
+def close_kernel(closes, nears, line, blank, plan_ref, after_ref, *refs):
+    refs, (sum_ref, right_ref, token_ref, left_ref, lists_ref, semaphore) = refs[:-6], refs[-6:]
+    copy = fetch(plan_ref, lists_ref, semaphore)
     sums, refs = refs[:2], refs[2:]
     lows, highs, refs = refs[:closes], refs[closes : 2 * closes], refs[2 * closes :]
     near_refs, refs = refs[:nears], refs[nears:]
@@ -278,19 +307,22 @@
     for s in range(sum_ref.shape[0]):
         both = [sums[0][s][:, :half], sums[1][s][:, :half]]
         sum_ref[s] = -1.5 * jnp.concatenate(both, axis=1)
-    add_products(plan_ref, total_ref, 2, left_ref, right_ref, sum_ref)
-
-
-def distant_kernel(distants, close, plan_ref, total_ref, close_ref, right_ref, *refs):
+    copy.wait()
+    add_products(lists_ref, 2, left_ref, right_ref, sum_ref)
+
+
+def distant_kernel(distants, start, plan_ref, close_ref, right_ref, *refs):
     lows, highs = refs[:distants], refs[distants : 2 * distants]
-    out_ref, left_ref, sum_ref = refs[-3:]
+    out_ref, left_ref, sum_ref, lists_ref, semaphore = refs[-5:]
+    copy = fetch(plan_ref, lists_ref, semaphore)
     at = 0
     for low_ref, high_ref in zip(lows, highs):
         join(left_ref, at, low_ref, high_ref, 0, 0, low_ref.shape[0])
         at += 2 * low_ref.shape[0]
     left_ref[at] = jnp.zeros(left_ref.shape[1:], left_ref.dtype)
     sum_ref[...] = close_ref[...]
-    add_products(plan_ref, total_ref, 3, left_ref, right_ref, sum_ref, close)
+    copy.wait()
+    add_products(lists_ref, 3, left_ref, right_ref, sum_ref, start)
     out_ref[...] = (-2.0 * sum_ref[...]).astype(jnp.bfloat16)
 
 
@@ -330,18 +362,23 @@
     extent = blocks.shape[-1]
     slots, terms = pairs.shape[2], pairs.shape[3]
     rows, cols = lax.axis_size("row"), lax.axis_size("col")
-    line = rows == 4
+    line = rows == 4 and cols > 1 and is_power(cols)
     local = blocks.reshape(slots, extent, extent)
     pairing = jnp.swapaxes(pairs.reshape(slots, terms, 2), 1, 2)
 
-    def call(kernel, outs, ins, scratch=(), smem=0, out_smem=False, us=2):
-        sizes = [(a.shape, a.dtype) for a in ins[smem:]] + [(a.shape, a.dtype) for a in scratch]
+    def call(kernel, outs, ins, scratch=(), smem=0, out_smem=False, us=2, plan=None):
+        if plan is not None:
+            ins = [plan, *ins]
+            scratch = [*scratch, pltpu.SMEM(plan.shape, plan.dtype), pltpu.SemaphoreType.DMA]
+        first = smem if plan is None else 1
+        sizes = [(a.shape, a.dtype) for a in ins[first:]]
+        sizes += [(a.shape, a.dtype) for a in (scratch if plan is None else scratch[:-2])]
         sizes += [] if out_smem else outs
         vmem = 4 * MIB + sum(math.prod(shape) * jnp.dtype(dtype).itemsize for shape, dtype in sizes)
         return pl.pallas_call(
             kernel,
             out_shape=[jax.ShapeDtypeStruct(shape, dtype) for shape, dtype in outs],
-            in_specs=[SMEM] * smem + [VMEM] * (len(ins) - smem),
+            in_specs=([SMEM] * smem if plan is None else [ANY]) + [VMEM] * (len(ins) - first),
             out_specs=[SMEM if out_smem else VMEM] * len(outs),
             scratch_shapes=list(scratch),
             compiler_params=params(vmem),
@@ -365,9 +402,9 @@
     far_count = 2 * CAP if line else rows * CAP
     right_count = near_count + far_count
     room = slots * terms + 4 * CHUNK
-    plan, total = call(
+    plan, planned = call(
         functools.partial(plan_kernel, near_count, close, blank),
-        [((4 * room,), jnp.int32), ((4,), jnp.int32)],
+        [((4 * room + LANES,), jnp.int32), ((4,), jnp.int32)],
         [table, term_count.reshape(1, slots)],
         smem=2,
         out_smem=True,
@@ -376,13 +413,25 @@
         outer = [(i, i ^ 1) for i in range(rows)]
         inner = [(1, 2), (2, 1)]
         partner = lax.ppermute(local, "row", outer)
-        middle = lax.ppermute(local, "row", inner)
+        ends = [row * cols + col for row in (0, 3) for col in range(cols)]
+        middles = [row * cols + col for row in (1, 2) for col in range(cols)]
+        other = [(i, i ^ (cols // 2)) for i in ends + middles]
+        middle = lax.ppermute(
+            local,
+            ("row", "col"),
+            [pair for pair in other if pair[0] in ends]
+            + [(i, 3 * cols + i % cols - i // cols * cols) for i in middles],
+        )
+        crossing = lax.ppermute(
+            local, ("row", "col"), [pair for pair in other if pair[0] in middles]
+        )
         asked = lax.ppermute(request, "row", outer)
-        halved = call(relay_kernel, [blocks_of(slots // 2)] * 2, [total, partner], smem=1)
+        halved = call(relay_kernel, [blocks_of(slots // 2)] * 2, [planned, partner], smem=1)
         passed = [lax.ppermute(piece, "row", inner) for piece in halved]
         (early,) = call(early_kernel, [blocks_of(CAP)], [asked, middle], smem=1)
         early = lax.ppermute(early, "row", outer)
         nears = [local, partner, middle]
+        crossing = call(choose_kernel, [blocks_of(slots // 2)] * 2, [middle, crossing, halved[0]])
         token = halved[0]
     else:
         asked = lax.all_to_all(request, "row", split_axis=0, concat_axis=0, tiled=True)
@@ -394,23 +443,29 @@
             for piece in picked
         ]
         far_panel = [fars[0][0], fars[1][0]]
-    lefts = row_panel(local, cols, token)
+    if line:
+        lefts = spread(local, cols // 2, cols)
+        for pieces in zip(*(spread(piece, cols // 2, cols) for piece in crossing)):
+            lefts += pieces
+    else:
+        lefts = row_panel(local, cols)
 
     def panel(count):
         return pltpu.VMEM((count, extent, extent), local.dtype)
 
-    near, left_panel, token = call(
+    near, left_panel, near_token = call(
         functools.partial(near_kernel, len(lefts)),
         [whole, blocks_of(blank + 1), ((8, LANES), jnp.float32)],
-        [plan, total, *lefts, *nears],
+        [*lefts, *nears],
         [panel(near_count)],
-        smem=2,
+        plan=plan,
+        us=0,
     )
     sums, squares, crossed, lates = [], [], [], []
     for turn in range(2):
         if line:
             (late,) = call(late_kernel, [blocks_of(CAP // 2)], [asked, passed[turn], token], smem=1)
-            token = late
+            token = near_token
             lates.append(lax.ppermute(late, "row", outer))
             far = [passed[turn], early, lates[turn]]
         else:
@@ -418,9 +473,9 @@
         total_half, stored = call(
             functools.partial(far_kernel, near_count, turn, line),
             [whole, blocks_of(slots // 2)],
-            [plan, total, near, left_panel, (squares or [near])[-1], *far],
+            [near, left_panel, (squares or [near])[-1], *far],
             [panel(right_count)],
-            smem=2,
+            plan=plan,
         )
         sums.append(total_half)
         squares.append(stored)
@@ -435,12 +490,12 @@
         crossed = squares
     if paired:
         crossed[0] = after(crossed[0], token, 0.3)
-    partial_sum, right_panel, token = call(
+    part, right_panel, token = call(
         functools.partial(close_kernel, len(closes[0]), len(nears), line, blank),
         [whole, blocks_of(right_count), ((8, LANES), jnp.float32)],
-        [plan, total, crossed[0], *sums, *closes[0], *closes[1], *nears, *far_panel],
+        [crossed[0], *sums, *closes[0], *closes[1], *nears, *far_panel],
         [panel(blank + 1)],
-        smem=2,
+        plan=plan,
         us=0,
     )
     distants = [[], []]
@@ -450,9 +505,9 @@
     (purified,) = call(
         functools.partial(distant_kernel, len(distants[0]), close),
         [((slots, extent, extent), local.dtype)],
-        [plan, total, partial_sum, right_panel, *distants[0], *distants[1]],
+        [part, right_panel, *distants[0], *distants[1]],
         [panel(blank + 1 - close), pltpu.VMEM(*whole)],
-        smem=2,
+        plan=plan,
     )
     return purified.reshape(blocks.shape)
 

time: 56.9 us -> 55.8 us (0.981)
  the two profiles are of different devices: /device:TPU:0 before, /device:TPU:13 now
where the time goes in v3:
time: 55.8 us; the launch traced here: 56.2 us
  Pallas kernels  21.6 us (39%)
  starting transfers between devices  20.9 us (37%)
  waiting for transfers between devices  12.7 us (23%)
  local copies, waits for them, and re-layouts  0.8 us (1%)
    pallas_call x12, Pallas kernels, call(): pl.pallas_call(kernel, out_shape=[jax.ShapeDtypeStruct(shape, dtype) for...  21.6 us
    ppermute x7, starting transfers between devices, spread(): lax.ppermute(pieces[k], 'col', [(i, i ^ bit) for i in range(cols)])  8.05 us
    ppermute x2, starting transfers between devices, per_device(): lax.ppermute(local, ('row', 'col'), [pair for pair in other if pair[0] in...  5.53 us
    ppermute x2, waiting for transfers between devices, cross(): lax.ppermute(blocks, 'col', [(i, i ^ cols // 2) for i in range(cols)])  4.24 us
    ppermute x2, starting transfers between devices, per_device(): passed = [lax.ppermute(piece, 'row', inner) for piece in halved]  3.84 us
    ppermute x2, waiting for transfers between devices, per_device(): lates.append(lax.ppermute(late, 'row', outer))  3.57 us
    ppermute x2, waiting for transfers between devices, per_device(): passed = [lax.ppermute(piece, 'row', inner) for piece in halved]  3.37 us
    ppermute x2, starting transfers between devices, cross(): lax.ppermute(blocks, 'col', [(i, i ^ cols // 2) for i in range(cols)])  1.79 us
  transfers between devices with their start and end apart: 18, of which 7 were waited for; matrix products, arithmetic and copies ran while one was open for 0% of the time, Pallas kernels for 33%

profile of v3, /device:TPU:13, one launch (start us, length us, event | category | flops | bytes accessed | tf_op | source)
XLA Modules:
  0.0 56.2 jit_solution(9535633152415230091)
XLA Ops:
  0.0 0.2 collective-permute-start.3
  0.2 2.4 %collective-permute-start.1 = (bf16[16,128,128]{2,1,0:T(8,128)(2,1)}, bf16[16,128,128]{2,1,0:T(8,128)(2,1)S(1)}, u32[]{:S(2)}, u32[]{:S(2)}) collective-permute-start(bf16[16,128,128]{2,1,0:T(8,128)(2,1)} %bitcast.7), channel_id=1, source_target_pairs={{0,2},{1,3},{2,0},{3,1},{12,14},{13,15},{14,12},{15,13},{4,8},{5,9... | collective-permute-start | bytes 1572872 | tf_op jit(solution)/shard_map/ppermute | solution.py:419
  2.6 3.1 %collective-permute-start.2 = (bf16[16,128,128]{2,1,0:T(8,128)(2,1)}, bf16[16,128,128]{2,1,0:T(8,128)(2,1)S(1)}, u32[]{:S(2)}, u32[]{:S(2)}) collective-permute-start(bf16[16,128,128]{2,1,0:T(8,128)(2,1)} %bitcast.8), channel_id=1, source_target_pairs={{4,6},{5,7},{6,4},{7,5},{8,10},{9,11},{10,8},{11,9},{20,22},{21,23... | collective-permute-start | bytes 1572872 | tf_op jit(solution)/shard_map/ppermute | solution.py:425
  5.7 1.6 %collective-permute-start = (bf16[16,128,128]{2,1,0:T(8,128)(2,1)}, bf16[16,128,128]{2,1,0:T(8,128)(2,1)S(1)}, u32[]{:S(2)}, u32[]{:S(2)}) collective-permute-start(bf16[16,128,128]{2,1,0:T(8,128)(2,1)} %bitcast.9), channel_id=1, source_target_pairs={{0,1},{1,0},{2,3},{3,2},{4,5},{5,4},{6,7},{7,6},{8,9},{9,8},{10,11... | collective-permute-start | bytes 1572872 | tf_op jit(solution)/shard_map/ppermute | solution.py:520
  7.3 0.7 %copy-done.1 = s32[1,1,16,16,2]{3,4,2,1,0:T(2,128)S(1)} copy-done((s32[1,1,16,16,2]{3,4,2,1,0:T(2,128)S(1)}, s32[1,1,16,16,2]{3,4,2,1,0:T(2,128)}, u32[]{:S(2)}) %copy-start.1) | copy-done | bytes 2072
  8.0 0.5 shard_map.37
  8.7 5.6 %shard_map.38 = (s32[1408]{0:T(1024)S(1)}, s32[4]{0:T(128)S(1)}) custom-call(s32[16,16]{1,0:T(8,128)S(1)} %get-tuple-element.23.table_ref, s32[1,16]{1,0:T(1,128)S(1)} %bitcast.14), custom_call_target="tpu_custom_call" | custom-call | flops 2000099968 | bytes 6001000 | tf_op jit(solution)/shard_map/pallas_call | solution.py:378
  14.3 0.8 %shard_map.39 = (bf16[8,128,128]{2,1,0:T(8,128)(2,1)S(1)}, bf16[8,128,128]{2,1,0:T(8,128)(2,1)S(1)}) custom-call(s32[4]{0:T(128)S(1)} %get-tuple-element.25.after_ref, bf16[16,128,128]{2,1,0:T(8,128)(2,1)S(1)} %collective-permute-done.3.partner_ref.refs_7_), custom_call_target="tpu_custom_call" | custom-call | flops 2000099968 | bytes 6001000 | tf_op jit(solution)/shard_map/pallas_call | solution.py:378
  15.0 1.9 %collective-permute-start.6 = (bf16[8,128,128]{2,1,0:T(8,128)(2,1)S(1)}, bf16[8,128,128]{2,1,0:T(8,128)(2,1)S(1)}, u32[]{:S(2)}, u32[]{:S(2)}) collective-permute-start(bf16[8,128,128]{2,1,0:T(8,128)(2,1)S(1)} %get-tuple-element.26.after_ref), channel_id=1, source_target_pairs={{4,8},{8,4},{5,9},{9,5},{6,10},{10,6},{7,11},{11,7},{20,24},{24,20... | collective-permute-start | bytes 786440 | tf_op jit(solution)/shard_map/ppermute | solution.py:430
  17.1 2.1 %collective-permute-start.4 = (bf16[8,128,128]{2,1,0:T(8,128)(2,1)S(1)}, bf16[8,128,128]{2,1,0:T(8,128)(2,1)S(1)}, u32[]{:S(2)}, u32[]{:S(2)}) collective-permute-start(bf16[8,128,128]{2,1,0:T(8,128)(2,1)S(1)} %get-tuple-element.27.refs_2_), channel_id=1, source_target_pairs={{0,1},{1,0},{2,3},{3,2},{4,5},{5,4},{6,7},{7,6},{8,9},{9,8},{10,11... | collective-permute-start | bytes 786440 | tf_op jit(solution)/shard_map/ppermute | solution.py:520
  19.1 0.1 collective-permute-start.5
  19.2 1.9 %collective-permute-start.11 = (bf16[8,128,128]{2,1,0:T(8,128)(2,1)S(1)}, bf16[8,128,128]{2,1,0:T(8,128)(2,1)S(1)}, u32[]{:S(2)}, u32[]{:S(2)}) collective-permute-start(bf16[8,128,128]{2,1,0:T(8,128)(2,1)S(1)} %get-tuple-element.35), channel_id=1, source_target_pairs={{4,8},{8,4},{5,9},{9,5},{6,10},{10,6},{7,11},{11,7},{20,24},{24,20... | collective-permute-start | bytes 786440 | tf_op jit(solution)/shard_map/ppermute | solution.py:430
  21.1 0.7 %shard_map.42 = bf16[8,128,128]{2,1,0:T(8,128)(2,1)S(1)} custom-call(s32[2,128]{1,0:T(2,128)S(1)} %collective-permute-done.7.asked_ref, bf16[16,128,128]{2,1,0:T(8,128)(2,1)S(1)} %collective-permute-done.1.ends_ref.refs_8_.middle_ref), custom_call_target="tpu_custom_call" | custom-call | flops 2000099968 | bytes 6001000 | tf_op jit(solution)/shard_map/pallas_call | solution.py:378
  21.8 2.7 %collective-permute-done.6.passed_ref.refs_0_.refs_9_ = bf16[8,128,128]{2,1,0:T(8,128)(2,1)S(1)} collective-permute-done((bf16[8,128,128]{2,1,0:T(8,128)(2,1)S(1)}, bf16[8,128,128]{2,1,0:T(8,128)(2,1)S(1)}, u32[]{:S(2)}, u32[]{:S(2)}) %collective-permute-start.6) | collective-permute-done | bytes 262176 | tf_op jit(solution)/shard_map/ppermute | solution.py:430
  24.6 0.8 %shard_map.43 = bf16[4,128,128]{2,1,0:T(8,128)(2,1)S(1)} custom-call(s32[2,128]{1,0:T(2,128)S(1)} %collective-permute-done.7.asked_ref, bf16[8,128,128]{2,1,0:T(8,128)(2,1)S(1)} %collective-permute-done.6.passed_ref.refs_0_.refs_9_, bf16[8,128,128]{2,1,0:T(8,128)(2,1)S(1)} %get-tuple-element.26.after_ref), custom_call_target="tpu_custom_call" | custom-call | flops 2000099968 | bytes 6001000 | tf_op jit(solution)/shard_map/pallas_call | solution.py:378
  25.3 1.3 %collective-permute-start.9 = (bf16[4,128,128]{2,1,0:T(8,128)(2,1)S(1)}, bf16[4,128,128]{2,1,0:T(8,128)(2,1)S(1)}, u32[]{:S(2)}, u32[]{:S(2)}) collective-permute-start(bf16[4,128,128]{2,1,0:T(8,128)(2,1)S(1)} %shard_map.43), channel_id=1, source_target_pairs={{0,4},{4,0},{8,12},{12,8},{1,5},{5,1},{9,13},{13,9},{2,6},{6,2},{1... | collective-permute-start | bytes 393224 | tf_op jit(solution)/shard_map/ppermute | solution.py:469
  26.7 2.8 %shard_map.41 = (f32[16,128,128]{2,1,0:T(8,128)S(1)}, bf16[65,128,128]{2,1,0:T(8,128)(2,1)S(1)}, f32[8,128]{1,0:T(8,128)S(1)}) custom-call(s32[1408]{0:T(1024)S(1)} %get-tuple-element.24.plan_ref, bf16[16,128,128]{2,1,0:T(8,128)(2,1)S(1)} %bitcast.10, bf16[16,128,128]{2,1,0:T(8,128)(2,1)S(1)} %collective-permute-done.refs_1_, ...), custom_call_target="tpu_custom_call" | custom-call | flops 100000 | bytes 1000 | tf_op jit(solution)/shard_map/pallas_call | solution.py:378
  29.5 0.7 %collective-permute-done.11.passed_ref.refs_0_.refs_10_ = bf16[8,128,128]{2,1,0:T(8,128)(2,1)S(1)} collective-permute-done((bf16[8,128,128]{2,1,0:T(8,128)(2,1)S(1)}, bf16[8,128,128]{2,1,0:T(8,128)(2,1)S(1)}, u32[]{:S(2)}, u32[]{:S(2)}) %collective-permute-start.11) | collective-permute-done | bytes 262176 | tf_op jit(solution)/shard_map/ppermute | solution.py:430
  30.2 0.8 %shard_map.46 = bf16[4,128,128]{2,1,0:T(8,128)(2,1)S(1)} custom-call(s32[2,128]{1,0:T(2,128)S(1)} %collective-permute-done.7.asked_ref, bf16[8,128,128]{2,1,0:T(8,128)(2,1)S(1)} %collective-permute-done.11.passed_ref.refs_0_.refs_10_, f32[8,128]{1,0:T(8,128)S(1)} %get-tuple-element.33.after_ref), custom_call_target="tpu_custom_call" | custom-call | flops 2000099968 | bytes 6001000 | tf_op jit(solution)/shard_map/pallas_call | solution.py:378
  31.0 2.3 %collective-permute-done.9.refs_2_.refs_12_ = bf16[4,128,128]{2,1,0:T(8,128)(2,1)S(1)} collective-permute-done((bf16[4,128,128]{2,1,0:T(8,128)(2,1)S(1)}, bf16[4,128,128]{2,1,0:T(8,128)(2,1)S(1)}, u32[]{:S(2)}, u32[]{:S(2)}) %collective-permute-start.9) | collective-permute-done | bytes 131104 | tf_op jit(solution)/shard_map/ppermute | solution.py:469
  33.4 1.9 %shard_map.44 = (f32[16,128,128]{2,1,0:T(8,128)S(1)}, bf16[8,128,128]{2,1,0:T(8,128)(2,1)S(1)}) custom-call(s32[1408]{0:T(1024)S(1)} %get-tuple-element.24.plan_ref, f32[16,128,128]{2,1,0:T(8,128)S(1)} %get-tuple-element.29.near_ref.after_ref, bf16[65,128,128]{2,1,0:T(8,128)(2,1)S(1)} %get-tuple-element.30.left_ref, ...), custom_call_target="tpu_custom_call" | custom-call | flops 2000099968 | bytes 6001000 | tf_op jit(solution)/shard_map/pallas_call | solution.py:378
  35.3 1.2 %collective-permute-done.12.refs_2_.refs_13_ = bf16[4,128,128]{2,1,0:T(8,128)(2,1)S(1)} collective-permute-done((bf16[4,128,128]{2,1,0:T(8,128)(2,1)S(1)}, bf16[4,128,128]{2,1,0:T(8,128)(2,1)S(1)}, u32[]{:S(2)}, u32[]{:S(2)}) %collective-permute-start.12) | collective-permute-done | bytes 131104 | tf_op jit(solution)/shard_map/ppermute | solution.py:469
  36.6 1.9 %shard_map.47 = (f32[16,128,128]{2,1,0:T(8,128)S(1)}, bf16[8,128,128]{2,1,0:T(8,128)(2,1)S(1)}) custom-call(s32[1408]{0:T(1024)S(1)} %get-tuple-element.24.plan_ref, f32[16,128,128]{2,1,0:T(8,128)S(1)} %get-tuple-element.29.near_ref.after_ref, bf16[65,128,128]{2,1,0:T(8,128)(2,1)S(1)} %get-tuple-element.30.left_ref, ...), custom_call_target="tpu_custom_call" | custom-call | flops 2000099968 | bytes 6001000 | tf_op jit(solution)/shard_map/pallas_call | solution.py:378
  38.5 3.0 %collective-permute-start.14 = (bf16[8,128,128]{2,1,0:T(8,128)(2,1)S(1)}, bf16[8,128,128]{2,1,0:T(8,128)(2,1)S(1)}, u32[]{:S(2)}, u32[]{:S(2)}) collective-permute-start(bf16[8,128,128]{2,1,0:T(8,128)(2,1)S(1)} %get-tuple-element.37.refs_4_), channel_id=1, source_target_pairs={{0,1},{1,0},{2,3},{3,2},{4,5},{5,4},{6,7},{7,6},{8,9},{9,8},{10,11... | collective-permute-start | bytes 786440 | tf_op jit(solution)/shard_map/ppermute | solution.py:520
  41.5 0.1 collective-permute-start.13
  41.6 1.7 %collective-permute-start.16 = (bf16[8,128,128]{2,1,0:T(8,128)(2,1)S(1)}, bf16[8,128,128]{2,1,0:T(8,128)(2,1)S(1)}, u32[]{:S(2)}, u32[]{:S(2)}) collective-permute-start(bf16[8,128,128]{2,1,0:T(8,128)(2,1)S(1)} %get-tuple-element.37.refs_4_), channel_id=1, source_target_pairs={{0,2},{1,3},{2,0},{3,1},{4,6},{5,7},{6,4},{7,5},{8,10},{9,11},{10,... | collective-permute-start | bytes 786440 | tf_op jit(solution)/shard_map/ppermute | solution.py:358
  43.3 2.7 %shard_map.48 = (f32[16,128,128]{2,1,0:T(8,128)S(1)}, bf16[64,128,128]{2,1,0:T(8,128)(2,1)S(1)}, f32[8,128]{1,0:T(8,128)S(1)}) custom-call(s32[1408]{0:T(1024)S(1)} %get-tuple-element.24.plan_ref, bf16[8,128,128]{2,1,0:T(8,128)(2,1)S(1)} %shard_map.45.after_ref.refs_0_, f32[16,128,128]{2,1,0:T(8,128)S(1)} %get-tuple-element.34.refs_0_, ...), custom_call_target="tpu_custom_call" | custom-call | flops 100000 | bytes 1000 | tf_op jit(solution)/shard_map/pallas_call | solution.py:378
  46.0 4.2 %collective-permute-done.16.value_ref = bf16[8,128,128]{2,1,0:T(8,128)(2,1)S(1)} collective-permute-done((bf16[8,128,128]{2,1,0:T(8,128)(2,1)S(1)}, bf16[8,128,128]{2,1,0:T(8,128)(2,1)S(1)}, u32[]{:S(2)}, u32[]{:S(2)}) %collective-permute-start.16) | collective-permute-done | bytes 262176 | tf_op jit(solution)/shard_map/ppermute | solution.py:358
  50.2 1.2 %collective-permute-start.17 = (bf16[8,128,128]{2,1,0:T(8,128)(2,1)S(1)}, bf16[8,128,128]{2,1,0:T(8,128)(2,1)S(1)}, u32[]{:S(2)}, u32[]{:S(2)}) collective-permute-start(bf16[8,128,128]{2,1,0:T(8,128)(2,1)S(1)} %shard_map.49.refs_2_), channel_id=1, source_target_pairs={{0,1},{1,0},{2,3},{3,2},{4,5},{5,4},{6,7},{7,6},{8,9},{9,8},{10,11... | collective-permute-start | bytes 786440 | tf_op jit(solution)/shard_map/ppermute | solution.py:520
  51.5 1.2 %collective-permute-done.17.refs_3_ = bf16[8,128,128]{2,1,0:T(8,128)(2,1)S(1)} collective-permute-done((bf16[8,128,128]{2,1,0:T(8,128)(2,1)S(1)}, bf16[8,128,128]{2,1,0:T(8,128)(2,1)S(1)}, u32[]{:S(2)}, u32[]{:S(2)}) %collective-permute-start.17) | collective-permute-done | bytes 262176 | tf_op jit(solution)/shard_map/ppermute | solution.py:520
  52.6 0.4 collective-permute-done.15.refs_1_
  53.0 3.3 %shard_map.50 = bf16[16,128,128]{2,1,0:T(8,128)(2,1)} custom-call(s32[1408]{0:T(1024)S(1)} %get-tuple-element.24.plan_ref, f32[16,128,128]{2,1,0:T(8,128)S(1)} %get-tuple-element.38.close_ref, bf16[64,128,128]{2,1,0:T(8,128)(2,1)S(1)} %get-tuple-element.39.right_ref, bf16[8,128,128]{2,1,0:T(8,128)(2,1)S(1)} %shard_map.45.after_ref.refs_0_, ...), custom_call_target="tpu_custom_call" | custom-call | flops 2000099968 | bytes 6001000 | tf_op jit(solution)/shard_map/pallas_call | solution.py:378
  (24 shorter events, 0.4 us)
Async XLA Ops:
  0.0 14.3 %collective-permute-start.3 = (bf16[16,128,128]{2,1,0:T(8,128)(2,1)}, bf16[16,128,128]{2,1,0:T(8,128)(2,1)S(1)}, u32[]{:S(2)}, u32[]{:S(2)}) collective-permute-start(bf16[16,128,128]{2,1,0:T(8,128)(2,1)} %bitcast.6), channel_id=1, source_target_pairs={{0,4},{4,0},{8,12},{12,8},{1,5},{5,1},{9,13},{13,9},{2,6},{6,2},{1... | collective-permute-start | bytes 1572872 | tf_op jit(solution)/shard_map/ppermute | solution.py:415
  0.2 16.8 %collective-permute-start.1 = (bf16[16,128,128]{2,1,0:T(8,128)(2,1)}, bf16[16,128,128]{2,1,0:T(8,128)(2,1)S(1)}, u32[]{:S(2)}, u32[]{:S(2)}) collective-permute-start(bf16[16,128,128]{2,1,0:T(8,128)(2,1)} %bitcast.7), channel_id=1, source_target_pairs={{0,2},{1,3},{2,0},{3,1},{12,14},{13,15},{14,12},{15,13},{4,8},{5,9... | collective-permute-start | bytes 1572872 | tf_op jit(solution)/shard_map/ppermute | solution.py:419
  2.6 14.4 %collective-permute-start.2 = (bf16[16,128,128]{2,1,0:T(8,128)(2,1)}, bf16[16,128,128]{2,1,0:T(8,128)(2,1)S(1)}, u32[]{:S(2)}, u32[]{:S(2)}) collective-permute-start(bf16[16,128,128]{2,1,0:T(8,128)(2,1)} %bitcast.8), channel_id=1, source_target_pairs={{4,6},{5,7},{6,4},{7,5},{8,10},{9,11},{10,8},{11,9},{20,22},{21,23... | collective-permute-start | bytes 1572872 | tf_op jit(solution)/shard_map/ppermute | solution.py:425
  5.7 19.6 %collective-permute-start = (bf16[16,128,128]{2,1,0:T(8,128)(2,1)}, bf16[16,128,128]{2,1,0:T(8,128)(2,1)S(1)}, u32[]{:S(2)}, u32[]{:S(2)}) collective-permute-start(bf16[16,128,128]{2,1,0:T(8,128)(2,1)} %bitcast.9), channel_id=1, source_target_pairs={{0,1},{1,0},{2,3},{3,2},{4,5},{5,4},{6,7},{7,6},{8,9},{9,8},{10,11... | collective-permute-start | bytes 1572872 | tf_op jit(solution)/shard_map/ppermute | solution.py:520
  7.3 0.7 %copy-start.1 = (s32[1,1,16,16,2]{3,4,2,1,0:T(2,128)S(1)}, s32[1,1,16,16,2]{3,4,2,1,0:T(2,128)}, u32[]{:S(2)}) copy-start(s32[1,1,16,16,2]{3,4,2,1,0:T(2,128)} %param.4) | copy-start | bytes 6148
  8.0 0.7 %copy-start.2 = (s32[1,1,16]{2,1,0:T(1,128)S(1)}, s32[1,1,16]{2,1,0:T(1,128)}, u32[]{:S(2)}) copy-start(s32[1,1,16]{2,1,0:T(1,128)} %param.5) | copy-start | bytes 196
  8.5 10.7 %collective-permute-start.7 = (s32[2,128]{1,0:T(2,128)S(1)}, s32[2,128]{1,0:T(2,128)S(1)}, u32[]{:S(2)}, u32[]{:S(2)}) collective-permute-start(s32[2,128]{1,0:T(2,128)S(1)} %get-tuple-element.31), channel_id=1, source_target_pairs={{0,4},{4,0},{8,12},{12,8},{1,5},{5,1},{9,13},{13,9},{2,6},{6,2},{1... | collective-permute-start | bytes 3080 | tf_op jit(solution)/shard_map/ppermute | solution.py:428
  15.0 9.5 %collective-permute-start.6 = (bf16[8,128,128]{2,1,0:T(8,128)(2,1)S(1)}, bf16[8,128,128]{2,1,0:T(8,128)(2,1)S(1)}, u32[]{:S(2)}, u32[]{:S(2)}) collective-permute-start(bf16[8,128,128]{2,1,0:T(8,128)(2,1)S(1)} %get-tuple-element.26.after_ref), channel_id=1, source_target_pairs={{4,8},{8,4},{5,9},{9,5},{6,10},{10,6},{7,11},{11,7},{20,24},{24,20... | collective-permute-start | bytes 786440 | tf_op jit(solution)/shard_map/ppermute | solution.py:430
  17.1 9.6 %collective-permute-start.4 = (bf16[8,128,128]{2,1,0:T(8,128)(2,1)S(1)}, bf16[8,128,128]{2,1,0:T(8,128)(2,1)S(1)}, u32[]{:S(2)}, u32[]{:S(2)}) collective-permute-start(bf16[8,128,128]{2,1,0:T(8,128)(2,1)S(1)} %get-tuple-element.27.refs_2_), channel_id=1, source_target_pairs={{0,1},{1,0},{2,3},{3,2},{4,5},{5,4},{6,7},{7,6},{8,9},{9,8},{10,11... | collective-permute-start | bytes 786440 | tf_op jit(solution)/shard_map/ppermute | solution.py:520
  19.1 7.5 %collective-permute-start.5 = (bf16[8,128,128]{2,1,0:T(8,128)(2,1)S(1)}, bf16[8,128,128]{2,1,0:T(8,128)(2,1)S(1)}, u32[]{:S(2)}, u32[]{:S(2)}) collective-permute-start(bf16[8,128,128]{2,1,0:T(8,128)(2,1)S(1)} %get-tuple-element.28.refs_3_), channel_id=1, source_target_pairs={{0,1},{1,0},{2,3},{3,2},{4,5},{5,4},{6,7},{7,6},{8,9},{9,8},{10,11... | collective-permute-start | bytes 786440 | tf_op jit(solution)/shard_map/ppermute | solution.py:520
  19.2 10.9 %collective-permute-start.11 = (bf16[8,128,128]{2,1,0:T(8,128)(2,1)S(1)}, bf16[8,128,128]{2,1,0:T(8,128)(2,1)S(1)}, u32[]{:S(2)}, u32[]{:S(2)}) collective-permute-start(bf16[8,128,128]{2,1,0:T(8,128)(2,1)S(1)} %get-tuple-element.35), channel_id=1, source_target_pairs={{4,8},{8,4},{5,9},{9,5},{6,10},{10,6},{7,11},{11,7},{20,24},{24,20... | collective-permute-start | bytes 786440 | tf_op jit(solution)/shard_map/ppermute | solution.py:430
  21.8 4.8 %copy-start = (bf16[1,1,16,128,128]{4,3,2,1,0:T(8,128)(2,1)S(1)}, bf16[1,1,16,128,128]{4,3,2,1,0:T(8,128)(2,1)}, u32[]{:S(2)}) copy-start(bf16[1,1,16,128,128]{4,3,2,1,0:T(8,128)(2,1)} %param.3) | copy-start | bytes 1572868
  24.5 6.5 %collective-permute-start.8 = (bf16[8,128,128]{2,1,0:T(8,128)(2,1)S(1)}, bf16[8,128,128]{2,1,0:T(8,128)(2,1)S(1)}, u32[]{:S(2)}, u32[]{:S(2)}) collective-permute-start(bf16[8,128,128]{2,1,0:T(8,128)(2,1)S(1)} %shard_map.42), channel_id=1, source_target_pairs={{0,4},{4,0},{8,12},{12,8},{1,5},{5,1},{9,13},{13,9},{2,6},{6,2},{1... | collective-permute-start | bytes 786440 | tf_op jit(solution)/shard_map/ppermute | solution.py:432
  25.3 8.0 %collective-permute-start.9 = (bf16[4,128,128]{2,1,0:T(8,128)(2,1)S(1)}, bf16[4,128,128]{2,1,0:T(8,128)(2,1)S(1)}, u32[]{:S(2)}, u32[]{:S(2)}) collective-permute-start(bf16[4,128,128]{2,1,0:T(8,128)(2,1)S(1)} %shard_map.43), channel_id=1, source_target_pairs={{0,4},{4,0},{8,12},{12,8},{1,5},{5,1},{9,13},{13,9},{2,6},{6,2},{1... | collective-permute-start | bytes 393224 | tf_op jit(solution)/shard_map/ppermute | solution.py:469
  30.9 5.6 %collective-permute-start.12 = (bf16[4,128,128]{2,1,0:T(8,128)(2,1)S(1)}, bf16[4,128,128]{2,1,0:T(8,128)(2,1)S(1)}, u32[]{:S(2)}, u32[]{:S(2)}) collective-permute-start(bf16[4,128,128]{2,1,0:T(8,128)(2,1)S(1)} %shard_map.46), channel_id=1, source_target_pairs={{0,4},{4,0},{8,12},{12,8},{1,5},{5,1},{9,13},{13,9},{2,6},{6,2},{1... | collective-permute-start | bytes 393224 | tf_op jit(solution)/shard_map/ppermute | solution.py:469
  35.3 8.0 %collective-permute-start.10 = (bf16[8,128,128]{2,1,0:T(8,128)(2,1)S(1)}, bf16[8,128,128]{2,1,0:T(8,128)(2,1)S(1)}, u32[]{:S(2)}, u32[]{:S(2)}) collective-permute-start(bf16[8,128,128]{2,1,0:T(8,128)(2,1)S(1)} %get-tuple-element.32.after_ref.refs_2_), channel_id=1, source_target_pairs={{0,2},{1,3},{2,0},{3,1},{4,6},{5,7},{6,4},{7,5},{8,10},{9,11},{10,... | collective-permute-start | bytes 786440 | tf_op jit(solution)/shard_map/ppermute | solution.py:358
  38.5 4.8 %collective-permute-start.14 = (bf16[8,128,128]{2,1,0:T(8,128)(2,1)S(1)}, bf16[8,128,128]{2,1,0:T(8,128)(2,1)S(1)}, u32[]{:S(2)}, u32[]{:S(2)}) collective-permute-start(bf16[8,128,128]{2,1,0:T(8,128)(2,1)S(1)} %get-tuple-element.37.refs_4_), channel_id=1, source_target_pairs={{0,1},{1,0},{2,3},{3,2},{4,5},{5,4},{6,7},{7,6},{8,9},{9,8},{10,11... | collective-permute-start | bytes 786440 | tf_op jit(solution)/shard_map/ppermute | solution.py:520
  41.5 1.8 %collective-permute-start.13 = (bf16[8,128,128]{2,1,0:T(8,128)(2,1)S(1)}, bf16[8,128,128]{2,1,0:T(8,128)(2,1)S(1)}, u32[]{:S(2)}, u32[]{:S(2)}) collective-permute-start(bf16[8,128,128]{2,1,0:T(8,128)(2,1)S(1)} %get-tuple-element.32.after_ref.refs_2_), channel_id=1, source_target_pairs={{0,1},{1,0},{2,3},{3,2},{4,5},{5,4},{6,7},{7,6},{8,9},{9,8},{10,11... | collective-permute-start | bytes 786440 | tf_op jit(solution)/shard_map/ppermute | solution.py:520
  41.6 8.6 %collective-permute-start.16 = (bf16[8,128,128]{2,1,0:T(8,128)(2,1)S(1)}, bf16[8,128,128]{2,1,0:T(8,128)(2,1)S(1)}, u32[]{:S(2)}, u32[]{:S(2)}) collective-permute-start(bf16[8,128,128]{2,1,0:T(8,128)(2,1)S(1)} %get-tuple-element.37.refs_4_), channel_id=1, source_target_pairs={{0,2},{1,3},{2,0},{3,1},{4,6},{5,7},{6,4},{7,5},{8,10},{9,11},{10,... | collective-permute-start | bytes 786440 | tf_op jit(solution)/shard_map/ppermute | solution.py:358
  50.2 2.4 %collective-permute-start.17 = (bf16[8,128,128]{2,1,0:T(8,128)(2,1)S(1)}, bf16[8,128,128]{2,1,0:T(8,128)(2,1)S(1)}, u32[]{:S(2)}, u32[]{:S(2)}) collective-permute-start(bf16[8,128,128]{2,1,0:T(8,128)(2,1)S(1)} %shard_map.49.refs_2_), channel_id=1, source_target_pairs={{0,1},{1,0},{2,3},{3,2},{4,5},{5,4},{6,7},{7,6},{8,9},{9,8},{10,11... | collective-permute-start | bytes 786440 | tf_op jit(solution)/shard_map/ppermute | solution.py:520
  51.5 1.5 %collective-permute-start.15 = (bf16[8,128,128]{2,1,0:T(8,128)(2,1)S(1)}, bf16[8,128,128]{2,1,0:T(8,128)(2,1)S(1)}, u32[]{:S(2)}, u32[]{:S(2)}) collective-permute-start(bf16[8,128,128]{2,1,0:T(8,128)(2,1)S(1)} %shard_map.45.after_ref.refs_0_), channel_id=1, source_target_pairs={{0,1},{1,0},{2,3},{3,2},{4,5},{5,4},{6,7},{7,6},{8,9},{9,8},{10,11... | collective-permute-start | bytes 786440 | tf_op jit(solution)/shard_map/ppermute | solution.py:520

commit v4 on v3

--- a/solution.py
+++ b/solution.py
@@ -202,23 +202,29 @@
 def add_products(lists_ref, which, left_ref, right_ref, sum_ref, start=0):
     room = room_of(lists_ref)
 
-    def step(c, carry):
-        for p in range(CHUNK):
-            first = lists_ref[which * room + 2 * (c * CHUNK + p)]
-            second = lists_ref[which * room + 2 * (c * CHUNK + p) + 1]
-            left = jnp.concatenate(
-                [left_ref[word % FIELD - start] for word in (first, second)], axis=1
-            )
-            right = jnp.concatenate(
-                [right_ref[(word // FIELD) % FIELD] for word in (first, second)], axis=0
-            )
-            sum_ref[first // (FIELD * FIELD)] += jnp.dot(
-                left, right, preferred_element_type=jnp.float32
-            )
-        return carry
+    def steps(pairs, at, count):
+        def step(c, carry):
+            for p in range(pairs):
+                entry = which * room + at + 2 * (c * pairs + p)
+                first, second = lists_ref[entry], lists_ref[entry + 1]
+                left = jnp.concatenate(
+                    [left_ref[word % FIELD - start] for word in (first, second)], axis=1
+                )
+                right = jnp.concatenate(
+                    [right_ref[(word // FIELD) % FIELD] for word in (first, second)], axis=0
+                )
+                sum_ref[first // (FIELD * FIELD)] += jnp.dot(
+                    left, right, preferred_element_type=jnp.float32
+                )
+            return carry
+
+        lax.fori_loop(0, count, step, 0)
 
     count = lists_ref[4 * room + which]
-    lax.fori_loop(0, (count + 2 * CHUNK - 1) // (2 * CHUNK), step, 0)
+    long_steps = count // (4 * CHUNK)
+    steps(2 * CHUNK, 0, long_steps)
+    done = long_steps * 4 * CHUNK
+    steps(CHUNK, done, (count - done + 2 * CHUNK - 1) // (2 * CHUNK))
 
 
 def near_kernel(lefts, plan_ref, *refs):
@@ -427,8 +433,10 @@
         )
         asked = lax.ppermute(request, "row", outer)
         halved = call(relay_kernel, [blocks_of(slots // 2)] * 2, [planned, partner], smem=1)
-        passed = [lax.ppermute(piece, "row", inner) for piece in halved]
         (early,) = call(early_kernel, [blocks_of(CAP)], [asked, middle], smem=1)
+        passed = [
+            lax.ppermute(piece, "row", inner) for piece in (halved[0], after(halved[1], early))
+        ]
         early = lax.ppermute(early, "row", outer)
         nears = [local, partner, middle]
         crossing = call(choose_kernel, [blocks_of(slots // 2)] * 2, [middle, crossing, halved[0]])

time: 55.8 us -> 54.4 us (0.975)
  the two profiles are of different devices: /device:TPU:13 before, /device:TPU:0 now
where the time goes in v4:
time: 54.4 us; the launch traced here: 54.1 us
  starting transfers between devices  25.5 us (47%)
  Pallas kernels  20.5 us (38%)
  waiting for transfers between devices  7.23 us (13%)
  local copies, waits for them, and re-layouts  0.72 us (1%)
    pallas_call x12, Pallas kernels, call(): pl.pallas_call(kernel, out_shape=[jax.ShapeDtypeStruct(shape, dtype) for...  20.5 us
    ppermute x1, starting transfers between devices, per_device(): early = lax.ppermute(early, 'row', outer)  7.16 us
    ppermute x2, waiting for transfers between devices, cross(): lax.ppermute(blocks, 'col', [(i, i ^ cols // 2) for i in range(cols)])  5.24 us
    ppermute x1, starting transfers between devices, per_device(): asked = lax.ppermute(request, 'row', outer)  4.43 us
    ppermute x2, starting transfers between devices, per_device(): lates.append(lax.ppermute(late, 'row', outer))  3.78 us
    ppermute x1, starting transfers between devices, per_device(): partner = lax.ppermute(local, 'row', outer)  3.02 us
    ppermute x2, starting transfers between devices, per_device(): lax.ppermute(local, ('row', 'col'), [pair for pair in other if pair[0] in...  2.17 us
    ppermute x7, starting transfers between devices, spread(): lax.ppermute(pieces[k], 'col', [(i, i ^ bit) for i in range(cols)])  1.72 us
  transfers between devices with their start and end apart: 18, of which 5 were waited for; matrix products, arithmetic and copies ran while one was open for 0% of the time, Pallas kernels for 32%

profile of v4, /device:TPU:0, one launch (start us, length us, event | category | flops | bytes accessed | tf_op | source)
XLA Modules:
  0.0 54.1 jit_solution(1613768623316236272)
XLA Ops:
  0.0 3.0 %collective-permute-start.3 = (bf16[16,128,128]{2,1,0:T(8,128)(2,1)}, bf16[16,128,128]{2,1,0:T(8,128)(2,1)S(1)}, u32[]{:S(2)}, u32[]{:S(2)}) collective-permute-start(bf16[16,128,128]{2,1,0:T(8,128)(2,1)} %bitcast.6), channel_id=1, source_target_pairs={{0,4},{4,0},{8,12},{12,8},{1,5},{5,1},{9,13},{13,9},{2,6},{6,2},{1... | collective-permute-start | bytes 1572872 | tf_op jit(solution)/shard_map/ppermute | solution.py:421
  3.0 1.5 %collective-permute-start.1 = (bf16[16,128,128]{2,1,0:T(8,128)(2,1)}, bf16[16,128,128]{2,1,0:T(8,128)(2,1)S(1)}, u32[]{:S(2)}, u32[]{:S(2)}) collective-permute-start(bf16[16,128,128]{2,1,0:T(8,128)(2,1)} %bitcast.7), channel_id=1, source_target_pairs={{0,2},{1,3},{2,0},{3,1},{12,14},{13,15},{14,12},{15,13},{4,8},{5,9... | collective-permute-start | bytes 1572872 | tf_op jit(solution)/shard_map/ppermute | solution.py:425
  4.5 0.7 %collective-permute-start.2 = (bf16[16,128,128]{2,1,0:T(8,128)(2,1)}, bf16[16,128,128]{2,1,0:T(8,128)(2,1)S(1)}, u32[]{:S(2)}, u32[]{:S(2)}) collective-permute-start(bf16[16,128,128]{2,1,0:T(8,128)(2,1)} %bitcast.8), channel_id=1, source_target_pairs={{4,6},{5,7},{6,4},{7,5},{8,10},{9,11},{10,8},{11,9},{20,22},{21,23... | collective-permute-start | bytes 1572872 | tf_op jit(solution)/shard_map/ppermute | solution.py:431
  5.2 0.1 collective-permute-start
  5.3 0.7 %copy-done.1 = s32[1,1,16,16,2]{3,4,2,1,0:T(2,128)S(1)} copy-done((s32[1,1,16,16,2]{3,4,2,1,0:T(2,128)S(1)}, s32[1,1,16,16,2]{3,4,2,1,0:T(2,128)}, u32[]{:S(2)}) %copy-start.1) | copy-done | bytes 2072
  6.0 0.5 shard_map.37
  6.5 4.4 %collective-permute-start.7 = (s32[2,128]{1,0:T(2,128)S(1)}, s32[2,128]{1,0:T(2,128)S(1)}, u32[]{:S(2)}, u32[]{:S(2)}) collective-permute-start(s32[2,128]{1,0:T(2,128)S(1)} %get-tuple-element.31), channel_id=1, source_target_pairs={{0,4},{4,0},{8,12},{12,8},{1,5},{5,1},{9,13},{13,9},{2,6},{6,2},{1... | collective-permute-start | bytes 3080 | tf_op jit(solution)/shard_map/ppermute | solution.py:434
  10.9 5.3 %shard_map.38 = (s32[1408]{0:T(1024)S(1)}, s32[4]{0:T(128)S(1)}) custom-call(s32[16,16]{1,0:T(8,128)S(1)} %get-tuple-element.23.table_ref, s32[1,16]{1,0:T(1,128)S(1)} %bitcast.14), custom_call_target="tpu_custom_call" | custom-call | flops 2000099968 | bytes 6001000 | tf_op jit(solution)/shard_map/pallas_call | solution.py:384
  16.2 0.6 %shard_map.39 = (bf16[8,128,128]{2,1,0:T(8,128)(2,1)S(1)}, bf16[8,128,128]{2,1,0:T(8,128)(2,1)S(1)}) custom-call(s32[4]{0:T(128)S(1)} %get-tuple-element.25.after_ref, bf16[16,128,128]{2,1,0:T(8,128)(2,1)S(1)} %collective-permute-done.3.partner_ref.refs_7_), custom_call_target="tpu_custom_call" | custom-call | flops 2000099968 | bytes 6001000 | tf_op jit(solution)/shard_map/pallas_call | solution.py:384
  16.8 0.7 %collective-permute-start.6 = (bf16[8,128,128]{2,1,0:T(8,128)(2,1)S(1)}, bf16[8,128,128]{2,1,0:T(8,128)(2,1)S(1)}, u32[]{:S(2)}, u32[]{:S(2)}) collective-permute-start(bf16[8,128,128]{2,1,0:T(8,128)(2,1)S(1)} %get-tuple-element.26.after_ref), channel_id=1, source_target_pairs={{4,8},{8,4},{5,9},{9,5},{6,10},{10,6},{7,11},{11,7},{20,24},{24,20... | collective-permute-start | bytes 786440 | tf_op jit(solution)/shard_map/ppermute | solution.py:438
  17.6 0.5 collective-permute-start.5
  18.1 0.6 %shard_map.42.after_ref = bf16[8,128,128]{2,1,0:T(8,128)(2,1)S(1)} custom-call(s32[2,128]{1,0:T(2,128)S(1)} %collective-permute-done.7.asked_ref, bf16[16,128,128]{2,1,0:T(8,128)(2,1)S(1)} %collective-permute-done.1.ends_ref.refs_8_.middle_ref), custom_call_target="tpu_custom_call" | custom-call | flops 2000099968 | bytes 6001000 | tf_op jit(solution)/shard_map/pallas_call | solution.py:384
  18.7 0.8 %collective-permute-start.11 = (bf16[8,128,128]{2,1,0:T(8,128)(2,1)S(1)}, bf16[8,128,128]{2,1,0:T(8,128)(2,1)S(1)}, u32[]{:S(2)}, u32[]{:S(2)}) collective-permute-start(bf16[8,128,128]{2,1,0:T(8,128)(2,1)S(1)} %shard_map.46), channel_id=1, source_target_pairs={{4,8},{8,4},{5,9},{9,5},{6,10},{10,6},{7,11},{11,7},{20,24},{24,20... | collective-permute-start | bytes 786440 | tf_op jit(solution)/shard_map/ppermute | solution.py:438
  19.6 7.2 %collective-permute-start.8 = (bf16[8,128,128]{2,1,0:T(8,128)(2,1)S(1)}, bf16[8,128,128]{2,1,0:T(8,128)(2,1)S(1)}, u32[]{:S(2)}, u32[]{:S(2)}) collective-permute-start(bf16[8,128,128]{2,1,0:T(8,128)(2,1)S(1)} %shard_map.42.after_ref), channel_id=1, source_target_pairs={{0,4},{4,0},{8,12},{12,8},{1,5},{5,1},{9,13},{13,9},{2,6},{6,2},{1... | collective-permute-start | bytes 786440 | tf_op jit(solution)/shard_map/ppermute | solution.py:440
  26.7 0.6 %shard_map.43 = bf16[4,128,128]{2,1,0:T(8,128)(2,1)S(1)} custom-call(s32[2,128]{1,0:T(2,128)S(1)} %collective-permute-done.7.asked_ref, bf16[8,128,128]{2,1,0:T(8,128)(2,1)S(1)} %collective-permute-done.6.passed_ref.refs_0_.refs_9_, bf16[8,128,128]{2,1,0:T(8,128)(2,1)S(1)} %get-tuple-element.26.after_ref), custom_call_target="tpu_custom_call" | custom-call | flops 2000099968 | bytes 6001000 | tf_op jit(solution)/shard_map/pallas_call | solution.py:384
  27.3 0.3 collective-permute-start.9
  27.6 2.2 %shard_map.41 = (f32[16,128,128]{2,1,0:T(8,128)S(1)}, bf16[65,128,128]{2,1,0:T(8,128)(2,1)S(1)}, f32[8,128]{1,0:T(8,128)S(1)}) custom-call(s32[1408]{0:T(1024)S(1)} %get-tuple-element.24.plan_ref, bf16[16,128,128]{2,1,0:T(8,128)(2,1)S(1)} %bitcast.10, bf16[16,128,128]{2,1,0:T(8,128)(2,1)S(1)} %collective-permute-done.refs_1_, ...), custom_call_target="tpu_custom_call" | custom-call | flops 100000 | bytes 1000 | tf_op jit(solution)/shard_map/pallas_call | solution.py:384
  29.8 0.6 %shard_map.47 = bf16[4,128,128]{2,1,0:T(8,128)(2,1)S(1)} custom-call(s32[2,128]{1,0:T(2,128)S(1)} %collective-permute-done.7.asked_ref, bf16[8,128,128]{2,1,0:T(8,128)(2,1)S(1)} %collective-permute-done.11.passed_ref.refs_0_.refs_10_, f32[8,128]{1,0:T(8,128)S(1)} %get-tuple-element.33.after_ref), custom_call_target="tpu_custom_call" | custom-call | flops 2000099968 | bytes 6001000 | tf_op jit(solution)/shard_map/pallas_call | solution.py:384
  30.3 3.5 %collective-permute-start.12 = (bf16[4,128,128]{2,1,0:T(8,128)(2,1)S(1)}, bf16[4,128,128]{2,1,0:T(8,128)(2,1)S(1)}, u32[]{:S(2)}, u32[]{:S(2)}) collective-permute-start(bf16[4,128,128]{2,1,0:T(8,128)(2,1)S(1)} %shard_map.47), channel_id=1, source_target_pairs={{0,4},{4,0},{8,12},{12,8},{1,5},{5,1},{9,13},{13,9},{2,6},{6,2},{1... | collective-permute-start | bytes 393224 | tf_op jit(solution)/shard_map/ppermute | solution.py:477
  33.9 0.6 %collective-permute-done.9.refs_2_.refs_12_ = bf16[4,128,128]{2,1,0:T(8,128)(2,1)S(1)} collective-permute-done((bf16[4,128,128]{2,1,0:T(8,128)(2,1)S(1)}, bf16[4,128,128]{2,1,0:T(8,128)(2,1)S(1)}, u32[]{:S(2)}, u32[]{:S(2)}) %collective-permute-start.9) | collective-permute-done | bytes 131104 | tf_op jit(solution)/shard_map/ppermute | solution.py:477
  34.4 2.3 %shard_map.44 = (f32[16,128,128]{2,1,0:T(8,128)S(1)}, bf16[8,128,128]{2,1,0:T(8,128)(2,1)S(1)}) custom-call(s32[1408]{0:T(1024)S(1)} %get-tuple-element.24.plan_ref, f32[16,128,128]{2,1,0:T(8,128)S(1)} %get-tuple-element.29.near_ref.after_ref, bf16[65,128,128]{2,1,0:T(8,128)(2,1)S(1)} %get-tuple-element.30.left_ref, ...), custom_call_target="tpu_custom_call" | custom-call | flops 2000099968 | bytes 6001000 | tf_op jit(solution)/shard_map/pallas_call | solution.py:384
  36.7 1.1 %collective-permute-start.10 = (bf16[8,128,128]{2,1,0:T(8,128)(2,1)S(1)}, bf16[8,128,128]{2,1,0:T(8,128)(2,1)S(1)}, u32[]{:S(2)}, u32[]{:S(2)}) collective-permute-start(bf16[8,128,128]{2,1,0:T(8,128)(2,1)S(1)} %get-tuple-element.32.after_ref.refs_2_), channel_id=1, source_target_pairs={{0,2},{1,3},{2,0},{3,1},{4,6},{5,7},{6,4},{7,5},{8,10},{9,11},{10,... | collective-permute-start | bytes 786440 | tf_op jit(solution)/shard_map/ppermute | solution.py:364
  37.9 2.3 %shard_map.48 = (f32[16,128,128]{2,1,0:T(8,128)S(1)}, bf16[8,128,128]{2,1,0:T(8,128)(2,1)S(1)}) custom-call(s32[1408]{0:T(1024)S(1)} %get-tuple-element.24.plan_ref, f32[16,128,128]{2,1,0:T(8,128)S(1)} %get-tuple-element.29.near_ref.after_ref, bf16[65,128,128]{2,1,0:T(8,128)(2,1)S(1)} %get-tuple-element.30.left_ref, ...), custom_call_target="tpu_custom_call" | custom-call | flops 2000099968 | bytes 6001000 | tf_op jit(solution)/shard_map/pallas_call | solution.py:384
  40.3 0.5 collective-permute-start.13
  40.8 0.5 collective-permute-start.16
  41.3 1.9 %collective-permute-done.10.value_ref = bf16[8,128,128]{2,1,0:T(8,128)(2,1)S(1)} collective-permute-done((bf16[8,128,128]{2,1,0:T(8,128)(2,1)S(1)}, bf16[8,128,128]{2,1,0:T(8,128)(2,1)S(1)}, u32[]{:S(2)}, u32[]{:S(2)}) %collective-permute-start.10) | collective-permute-done | bytes 262176 | tf_op jit(solution)/shard_map/ppermute | solution.py:364
  43.2 2.5 %shard_map.49 = (f32[16,128,128]{2,1,0:T(8,128)S(1)}, bf16[64,128,128]{2,1,0:T(8,128)(2,1)S(1)}, f32[8,128]{1,0:T(8,128)S(1)}) custom-call(s32[1408]{0:T(1024)S(1)} %get-tuple-element.24.plan_ref, bf16[8,128,128]{2,1,0:T(8,128)(2,1)S(1)} %shard_map.45.after_ref.refs_0_, f32[16,128,128]{2,1,0:T(8,128)S(1)} %get-tuple-element.34.refs_0_, ...), custom_call_target="tpu_custom_call" | custom-call | flops 100000 | bytes 1000 | tf_op jit(solution)/shard_map/pallas_call | solution.py:384
  45.7 3.4 %collective-permute-done.16.value_ref = bf16[8,128,128]{2,1,0:T(8,128)(2,1)S(1)} collective-permute-done((bf16[8,128,128]{2,1,0:T(8,128)(2,1)S(1)}, bf16[8,128,128]{2,1,0:T(8,128)(2,1)S(1)}, u32[]{:S(2)}, u32[]{:S(2)}) %collective-permute-start.16) | collective-permute-done | bytes 262176 | tf_op jit(solution)/shard_map/ppermute | solution.py:364
  49.1 0.5 collective-permute-start.15
  49.6 1.0 %collective-permute-done.17.refs_3_ = bf16[8,128,128]{2,1,0:T(8,128)(2,1)S(1)} collective-permute-done((bf16[8,128,128]{2,1,0:T(8,128)(2,1)S(1)}, bf16[8,128,128]{2,1,0:T(8,128)(2,1)S(1)}, u32[]{:S(2)}, u32[]{:S(2)}) %collective-permute-start.17) | collective-permute-done | bytes 262176 | tf_op jit(solution)/shard_map/ppermute | solution.py:528
  50.6 0.4 collective-permute-done.15.refs_1_
  51.0 3.1 %shard_map.51 = bf16[16,128,128]{2,1,0:T(8,128)(2,1)} custom-call(s32[1408]{0:T(1024)S(1)} %get-tuple-element.24.plan_ref, f32[16,128,128]{2,1,0:T(8,128)S(1)} %get-tuple-element.38.close_ref, bf16[64,128,128]{2,1,0:T(8,128)(2,1)S(1)} %get-tuple-element.39.right_ref, bf16[8,128,128]{2,1,0:T(8,128)(2,1)S(1)} %shard_map.45.after_ref.refs_0_, ...), custom_call_target="tpu_custom_call" | custom-call | flops 2000099968 | bytes 6001000 | tf_op jit(solution)/shard_map/pallas_call | solution.py:384
  (25 shorter events, 0.2 us)
Async XLA Ops:
  0.0 16.2 %collective-permute-start.3 = (bf16[16,128,128]{2,1,0:T(8,128)(2,1)}, bf16[16,128,128]{2,1,0:T(8,128)(2,1)S(1)}, u32[]{:S(2)}, u32[]{:S(2)}) collective-permute-start(bf16[16,128,128]{2,1,0:T(8,128)(2,1)} %bitcast.6), channel_id=1, source_target_pairs={{0,4},{4,0},{8,12},{12,8},{1,5},{5,1},{9,13},{13,9},{2,6},{6,2},{1... | collective-permute-start | bytes 1572872 | tf_op jit(solution)/shard_map/ppermute | solution.py:421
  3.0 14.5 %collective-permute-start.1 = (bf16[16,128,128]{2,1,0:T(8,128)(2,1)}, bf16[16,128,128]{2,1,0:T(8,128)(2,1)S(1)}, u32[]{:S(2)}, u32[]{:S(2)}) collective-permute-start(bf16[16,128,128]{2,1,0:T(8,128)(2,1)} %bitcast.7), channel_id=1, source_target_pairs={{0,2},{1,3},{2,0},{3,1},{12,14},{13,15},{14,12},{15,13},{4,8},{5,9... | collective-permute-start | bytes 1572872 | tf_op jit(solution)/shard_map/ppermute | solution.py:425
  4.5 13.0 %collective-permute-start.2 = (bf16[16,128,128]{2,1,0:T(8,128)(2,1)}, bf16[16,128,128]{2,1,0:T(8,128)(2,1)S(1)}, u32[]{:S(2)}, u32[]{:S(2)}) collective-permute-start(bf16[16,128,128]{2,1,0:T(8,128)(2,1)} %bitcast.8), channel_id=1, source_target_pairs={{4,6},{5,7},{6,4},{7,5},{8,10},{9,11},{10,8},{11,9},{20,22},{21,23... | collective-permute-start | bytes 1572872 | tf_op jit(solution)/shard_map/ppermute | solution.py:431
  5.2 22.1 %collective-permute-start = (bf16[16,128,128]{2,1,0:T(8,128)(2,1)}, bf16[16,128,128]{2,1,0:T(8,128)(2,1)S(1)}, u32[]{:S(2)}, u32[]{:S(2)}) collective-permute-start(bf16[16,128,128]{2,1,0:T(8,128)(2,1)} %bitcast.9), channel_id=1, source_target_pairs={{0,1},{1,0},{2,3},{3,2},{4,5},{5,4},{6,7},{7,6},{8,9},{9,8},{10,11... | collective-permute-start | bytes 1572872 | tf_op jit(solution)/shard_map/ppermute | solution.py:528
  5.3 0.7 %copy-start.1 = (s32[1,1,16,16,2]{3,4,2,1,0:T(2,128)S(1)}, s32[1,1,16,16,2]{3,4,2,1,0:T(2,128)}, u32[]{:S(2)}) copy-start(s32[1,1,16,16,2]{3,4,2,1,0:T(2,128)} %param.4) | copy-start | bytes 6148
  6.0 4.9 %copy-start.2 = (s32[1,1,16]{2,1,0:T(1,128)S(1)}, s32[1,1,16]{2,1,0:T(1,128)}, u32[]{:S(2)}) copy-start(s32[1,1,16]{2,1,0:T(1,128)} %param.5) | copy-start | bytes 196
  6.5 11.6 %collective-permute-start.7 = (s32[2,128]{1,0:T(2,128)S(1)}, s32[2,128]{1,0:T(2,128)S(1)}, u32[]{:S(2)}, u32[]{:S(2)}) collective-permute-start(s32[2,128]{1,0:T(2,128)S(1)} %get-tuple-element.31), channel_id=1, source_target_pairs={{0,4},{4,0},{8,12},{12,8},{1,5},{5,1},{9,13},{13,9},{2,6},{6,2},{1... | collective-permute-start | bytes 3080 | tf_op jit(solution)/shard_map/ppermute | solution.py:434
  16.8 2.8 %collective-permute-start.6 = (bf16[8,128,128]{2,1,0:T(8,128)(2,1)S(1)}, bf16[8,128,128]{2,1,0:T(8,128)(2,1)S(1)}, u32[]{:S(2)}, u32[]{:S(2)}) collective-permute-start(bf16[8,128,128]{2,1,0:T(8,128)(2,1)S(1)} %get-tuple-element.26.after_ref), channel_id=1, source_target_pairs={{4,8},{8,4},{5,9},{9,5},{6,10},{10,6},{7,11},{11,7},{20,24},{24,20... | collective-permute-start | bytes 786440 | tf_op jit(solution)/shard_map/ppermute | solution.py:438
  17.6 10.0 %collective-permute-start.4 = (bf16[8,128,128]{2,1,0:T(8,128)(2,1)S(1)}, bf16[8,128,128]{2,1,0:T(8,128)(2,1)S(1)}, u32[]{:S(2)}, u32[]{:S(2)}) collective-permute-start(bf16[8,128,128]{2,1,0:T(8,128)(2,1)S(1)} %get-tuple-element.27.refs_2_), channel_id=1, source_target_pairs={{0,1},{1,0},{2,3},{3,2},{4,5},{5,4},{6,7},{7,6},{8,9},{9,8},{10,11... | collective-permute-start | bytes 786440 | tf_op jit(solution)/shard_map/ppermute | solution.py:528
  17.6 9.9 %collective-permute-start.5 = (bf16[8,128,128]{2,1,0:T(8,128)(2,1)S(1)}, bf16[8,128,128]{2,1,0:T(8,128)(2,1)S(1)}, u32[]{:S(2)}, u32[]{:S(2)}) collective-permute-start(bf16[8,128,128]{2,1,0:T(8,128)(2,1)S(1)} %get-tuple-element.28.refs_3_), channel_id=1, source_target_pairs={{0,1},{1,0},{2,3},{3,2},{4,5},{5,4},{6,7},{7,6},{8,9},{9,8},{10,11... | collective-permute-start | bytes 786440 | tf_op jit(solution)/shard_map/ppermute | solution.py:528
  18.7 8.8 %copy-start = (bf16[1,1,16,128,128]{4,3,2,1,0:T(8,128)(2,1)S(1)}, bf16[1,1,16,128,128]{4,3,2,1,0:T(8,128)(2,1)}, u32[]{:S(2)}) copy-start(bf16[1,1,16,128,128]{4,3,2,1,0:T(8,128)(2,1)} %param.3) | copy-start | bytes 1572868
  18.7 11.0 %collective-permute-start.11 = (bf16[8,128,128]{2,1,0:T(8,128)(2,1)S(1)}, bf16[8,128,128]{2,1,0:T(8,128)(2,1)S(1)}, u32[]{:S(2)}, u32[]{:S(2)}) collective-permute-start(bf16[8,128,128]{2,1,0:T(8,128)(2,1)S(1)} %shard_map.46), channel_id=1, source_target_pairs={{4,8},{8,4},{5,9},{9,5},{6,10},{10,6},{7,11},{11,7},{20,24},{24,20... | collective-permute-start | bytes 786440 | tf_op jit(solution)/shard_map/ppermute | solution.py:438
  19.6 14.3 %collective-permute-start.8 = (bf16[8,128,128]{2,1,0:T(8,128)(2,1)S(1)}, bf16[8,128,128]{2,1,0:T(8,128)(2,1)S(1)}, u32[]{:S(2)}, u32[]{:S(2)}) collective-permute-start(bf16[8,128,128]{2,1,0:T(8,128)(2,1)S(1)} %shard_map.42.after_ref), channel_id=1, source_target_pairs={{0,4},{4,0},{8,12},{12,8},{1,5},{5,1},{9,13},{13,9},{2,6},{6,2},{1... | collective-permute-start | bytes 786440 | tf_op jit(solution)/shard_map/ppermute | solution.py:440
  27.3 7.1 %collective-permute-start.9 = (bf16[4,128,128]{2,1,0:T(8,128)(2,1)S(1)}, bf16[4,128,128]{2,1,0:T(8,128)(2,1)S(1)}, u32[]{:S(2)}, u32[]{:S(2)}) collective-permute-start(bf16[4,128,128]{2,1,0:T(8,128)(2,1)S(1)} %shard_map.43), channel_id=1, source_target_pairs={{0,4},{4,0},{8,12},{12,8},{1,5},{5,1},{9,13},{13,9},{2,6},{6,2},{1... | collective-permute-start | bytes 393224 | tf_op jit(solution)/shard_map/ppermute | solution.py:477
  30.3 7.5 %collective-permute-start.12 = (bf16[4,128,128]{2,1,0:T(8,128)(2,1)S(1)}, bf16[4,128,128]{2,1,0:T(8,128)(2,1)S(1)}, u32[]{:S(2)}, u32[]{:S(2)}) collective-permute-start(bf16[4,128,128]{2,1,0:T(8,128)(2,1)S(1)} %shard_map.47), channel_id=1, source_target_pairs={{0,4},{4,0},{8,12},{12,8},{1,5},{5,1},{9,13},{13,9},{2,6},{6,2},{1... | collective-permute-start | bytes 393224 | tf_op jit(solution)/shard_map/ppermute | solution.py:477
  36.7 6.4 %collective-permute-start.10 = (bf16[8,128,128]{2,1,0:T(8,128)(2,1)S(1)}, bf16[8,128,128]{2,1,0:T(8,128)(2,1)S(1)}, u32[]{:S(2)}, u32[]{:S(2)}) collective-permute-start(bf16[8,128,128]{2,1,0:T(8,128)(2,1)S(1)} %get-tuple-element.32.after_ref.refs_2_), channel_id=1, source_target_pairs={{0,2},{1,3},{2,0},{3,1},{4,6},{5,7},{6,4},{7,5},{8,10},{9,11},{10,... | collective-permute-start | bytes 786440 | tf_op jit(solution)/shard_map/ppermute | solution.py:364
  40.2 3.0 %collective-permute-start.14 = (bf16[8,128,128]{2,1,0:T(8,128)(2,1)S(1)}, bf16[8,128,128]{2,1,0:T(8,128)(2,1)S(1)}, u32[]{:S(2)}, u32[]{:S(2)}) collective-permute-start(bf16[8,128,128]{2,1,0:T(8,128)(2,1)S(1)} %get-tuple-element.37.refs_4_), channel_id=1, source_target_pairs={{0,1},{1,0},{2,3},{3,2},{4,5},{5,4},{6,7},{7,6},{8,9},{9,8},{10,11... | collective-permute-start | bytes 786440 | tf_op jit(solution)/shard_map/ppermute | solution.py:528
  40.3 2.9 %collective-permute-start.13 = (bf16[8,128,128]{2,1,0:T(8,128)(2,1)S(1)}, bf16[8,128,128]{2,1,0:T(8,128)(2,1)S(1)}, u32[]{:S(2)}, u32[]{:S(2)}) collective-permute-start(bf16[8,128,128]{2,1,0:T(8,128)(2,1)S(1)} %get-tuple-element.32.after_ref.refs_2_), channel_id=1, source_target_pairs={{0,1},{1,0},{2,3},{3,2},{4,5},{5,4},{6,7},{7,6},{8,9},{9,8},{10,11... | collective-permute-start | bytes 786440 | tf_op jit(solution)/shard_map/ppermute | solution.py:528
  40.8 8.3 %collective-permute-start.16 = (bf16[8,128,128]{2,1,0:T(8,128)(2,1)S(1)}, bf16[8,128,128]{2,1,0:T(8,128)(2,1)S(1)}, u32[]{:S(2)}, u32[]{:S(2)}) collective-permute-start(bf16[8,128,128]{2,1,0:T(8,128)(2,1)S(1)} %get-tuple-element.37.refs_4_), channel_id=1, source_target_pairs={{0,2},{1,3},{2,0},{3,1},{4,6},{5,7},{6,4},{7,5},{8,10},{9,11},{10,... | collective-permute-start | bytes 786440 | tf_op jit(solution)/shard_map/ppermute | solution.py:364
  49.1 1.5 %collective-permute-start.17 = (bf16[8,128,128]{2,1,0:T(8,128)(2,1)S(1)}, bf16[8,128,128]{2,1,0:T(8,128)(2,1)S(1)}, u32[]{:S(2)}, u32[]{:S(2)}) collective-permute-start(bf16[8,128,128]{2,1,0:T(8,128)(2,1)S(1)} %shard_map.50.refs_2_), channel_id=1, source_target_pairs={{0,1},{1,0},{2,3},{3,2},{4,5},{5,4},{6,7},{7,6},{8,9},{9,8},{10,11... | collective-permute-start | bytes 786440 | tf_op jit(solution)/shard_map/ppermute | solution.py:528
  49.1 1.9 %collective-permute-start.15 = (bf16[8,128,128]{2,1,0:T(8,128)(2,1)S(1)}, bf16[8,128,128]{2,1,0:T(8,128)(2,1)S(1)}, u32[]{:S(2)}, u32[]{:S(2)}) collective-permute-start(bf16[8,128,128]{2,1,0:T(8,128)(2,1)S(1)} %shard_map.45.after_ref.refs_0_), channel_id=1, source_target_pairs={{0,1},{1,0},{2,3},{3,2},{4,5},{5,4},{6,7},{7,6},{8,9},{9,8},{10,11... | collective-permute-start | bytes 786440 | tf_op jit(solution)/shard_map/ppermute | solution.py:528
